TPU v7x, 256 devices: a whole 4x4x8 slice. The times are simulated.
256 devices in a mesh: ctx: 32 (over x_lo, z, core), head: 8 (over x_hi, y).
Axes of the slice: x: 4 (x_hi: 2, x_lo: 2; x = x_hi * 2 + x_lo), y: 4, z: 8, core: 2. Of those that a mesh axis runs over, the one named last changes fastest.
Arguments:
- queries: bfloat16 [8192, 8192], P('ctx', 'head'), may hold values from -6 to 6
- keys: bfloat16 [8192, 1024], P('ctx', 'head'), may hold values from -6 to 6
- values: bfloat16 [8192, 1024], P('ctx', 'head'), may hold values from -6 to 6
- doc_lengths: int32 [16], replicated, may hold values from 1 to 4096, 8192 in all
- span_order: int32 [64], replicated, may hold values from 0 to 63, each once
Outputs:
- attended: bfloat16 [8192, 8192], P(('ctx', 'head'))
Inputs may be any that keep to these rules, and one draw needn't show every extreme that they name: `doc_lengths`: every document has at least one token and they fill the sequence; the longest has exactly 4096. `span_order`: each span appears in exactly one slot.
All inputs are finite; a program needn't handle non-finite values.
Results may differ from a plain program's by a relative error of at most 0.004.
Values may be sent and summed in bfloat16 or wider, within the bound.
A program may use at most 192 MiB of HBM per device.

v0:
```python
import math

import jax
import jax.numpy as jnp
from jax import lax
from jax.sharding import PartitionSpec as P

HD = 128


def shifted(block, axis, distance):
    devices = range(lax.axis_size(axis))
    route = [((i - distance) % len(devices), i) for i in devices]
    return lax.ppermute(block, axis, route)


def positions_of(first_row, count, span_order, span):
    rows = first_row + jnp.arange(count, dtype=jnp.int32)
    slots = rows // span
    nchunk = span_order.shape[0]
    table = jnp.sum(
        jnp.where(
            slots[:, None] == jnp.arange(nchunk, dtype=jnp.int32)[None, :], span_order[None, :], 0
        ),
        axis=1,
    )
    return table * span + rows % span


def documents_of(pos, ends):
    return jnp.sum((pos[:, None] >= ends[None, :]).astype(jnp.int32), axis=1)


def body(queries, keys, values, doc_lengths, span_order):
    tok_rows = queries.shape[0]
    span = tok_rows // 2
    heads_here = queries.shape[1] // HD
    kv_here = keys.shape[1] // HD
    group_size = heads_here // kv_here
    ctx_index = lax.axis_index("ctx")
    n_ctx = lax.axis_size("ctx")
    scale = 1.0 / math.sqrt(HD)
    ends = jnp.cumsum(doc_lengths)
    q_pos = positions_of(ctx_index * tok_rows, tok_rows, span_order, span)
    q_doc = documents_of(q_pos, ends)
    q_local = queries.reshape(tok_rows, kv_here, group_size, HD)

    def attend(state, key_piece, val_piece, allowed):
        top, total, accum = state
        key_heads = key_piece.reshape(key_piece.shape[0], kv_here, HD)
        val_heads = val_piece.reshape(val_piece.shape[0], kv_here, HD)
        score = (
            jnp.einsum("qcgd,kcd->cgqk", q_local, key_heads, preferred_element_type=jnp.float32)
            * scale
        )
        masked = jnp.where(allowed[None, None], score, -1e30)
        new_top = jnp.maximum(top, jnp.max(masked, axis=-1))
        weight = jnp.where(allowed[None, None], jnp.exp(score - new_top[..., None]), 0.0)
        factor = jnp.exp(top - new_top)
        total = total * factor + jnp.sum(weight, axis=-1)
        weight_b = weight.astype(jnp.bfloat16)
        accum = accum * factor[..., None] + jnp.einsum(
            "cgqk,kcd->cgqd", weight_b, val_heads, preferred_element_type=jnp.float32
        )
        return (new_top, total, accum)

    def fold_block(state, pieces, start):
        key_piece, val_piece = pieces
        k_pos = positions_of(start, key_piece.shape[0], span_order, span)
        k_doc = documents_of(k_pos, ends)
        allowed = (q_doc[:, None] == k_doc[None, :]) & (k_pos[None, :] <= q_pos[:, None])
        return attend(state, key_piece, val_piece, allowed)

    initial = (
        jnp.full((kv_here, group_size, tok_rows), -1e30, jnp.float32),
        jnp.zeros((kv_here, group_size, tok_rows), jnp.float32),
        jnp.zeros((kv_here, group_size, tok_rows, HD), jnp.float32),
    )

    def circle_step(step, carry):
        state, key_blk, val_blk = carry
        source = (ctx_index - step + n_ctx) % n_ctx
        state = fold_block(state, (key_blk, val_blk), source * tok_rows)
        key_blk, val_blk = shifted((key_blk, val_blk), "ctx", 1)
        return (state, key_blk, val_blk)

    state, key_blk, val_blk = lax.fori_loop(0, n_ctx - 1, circle_step, (initial, keys, values))
    source = (ctx_index + 1) % n_ctx
    state = fold_block(state, (key_blk, val_blk), source * tok_rows)
    top, total, accum = state
    result = accum / total[..., None]
    local_out = (
        jnp.transpose(result, (2, 0, 1, 3)).reshape(tok_rows, heads_here * HD).astype(jnp.bfloat16)
    )
    return lax.all_to_all(local_out, "head", split_axis=0, concat_axis=1, tiled=True)


def solution(mesh):
    return jax.shard_map(
        body,
        mesh=mesh,
        in_specs=(P("ctx", "head"), P("ctx", "head"), P("ctx", "head"), P(), P()),
        out_specs=P(("ctx", "head"), None),
        check_vma=False,
    )
```

profile of v0, /device:TPU:30, one launch (start us, length us, event | category | flops | bytes accessed | tf_op | source)
XLA Modules:
  0.0 222.9 jit_solution(16497237106857679866)
XLA Ops:
  1.0 1.2 copy.27
  2.9 203.6 %while.25 = (s32[]{:T(128)}, f32[1,8,256]{2,1,0:T(8,128)S(1)}, f32[1,8,256]{2,1,0:T(8,128)S(1)}, f32[1,8,256,128]{3,2,1,0:T(8,128)S(1)}, bf16[256,128]{1,0:T(8,1...) while((s32[]{:T(128)}, f32[1,8,256]{2,1,0:T(8,128)S(1)}, ...), condition=%wide.region_8.9_spmd.clone, body=%wide.region_3.8_spmd.clone.sunk | while | flops 275266560 | bytes 10235602 | solution.py:87
  3.0 2.0 collective-permute-start.1
  6.3 0.9 fusion.64
  7.3 3.2 %collective-permute-done = bf16[256,128]{1,0:T(8,128)(2,1)S(1)} collective-permute-done((bf16[256,128]{1,0:T(8,128)(2,1)S(1)}, bf16[256,128]{1,0:T(8,128)(2,1)S(1)}, u32[]{:S(2)}, u32[]{:S(2)}) %collective-permute-start) | collective-permute-done | bytes 65568 | tf_op jit(solution)/shard_map/while/body/eval_jaxpr/ppermute | solution.py:14
  12.7 0.9 fusion.64
  13.6 3.4 %collective-permute-done = bf16[256,128]{1,0:T(8,128)(2,1)S(1)} collective-permute-done((bf16[256,128]{1,0:T(8,128)(2,1)S(1)}, bf16[256,128]{1,0:T(8,128)(2,1)S(1)}, u32[]{:S(2)}, u32[]{:S(2)}) %collective-permute-start) | collective-permute-done | bytes 65568 | tf_op jit(solution)/shard_map/while/body/eval_jaxpr/ppermute | solution.py:14
  19.2 0.9 fusion.64
  20.1 3.4 %collective-permute-done = bf16[256,128]{1,0:T(8,128)(2,1)S(1)} collective-permute-done((bf16[256,128]{1,0:T(8,128)(2,1)S(1)}, bf16[256,128]{1,0:T(8,128)(2,1)S(1)}, u32[]{:S(2)}, u32[]{:S(2)}) %collective-permute-start) | collective-permute-done | bytes 65568 | tf_op jit(solution)/shard_map/while/body/eval_jaxpr/ppermute | solution.py:14
  25.7 0.9 fusion.64
  26.7 3.4 %collective-permute-done = bf16[256,128]{1,0:T(8,128)(2,1)S(1)} collective-permute-done((bf16[256,128]{1,0:T(8,128)(2,1)S(1)}, bf16[256,128]{1,0:T(8,128)(2,1)S(1)}, u32[]{:S(2)}, u32[]{:S(2)}) %collective-permute-start) | collective-permute-done | bytes 65568 | tf_op jit(solution)/shard_map/while/body/eval_jaxpr/ppermute | solution.py:14
  32.2 0.9 fusion.64
  33.2 3.4 %collective-permute-done = bf16[256,128]{1,0:T(8,128)(2,1)S(1)} collective-permute-done((bf16[256,128]{1,0:T(8,128)(2,1)S(1)}, bf16[256,128]{1,0:T(8,128)(2,1)S(1)}, u32[]{:S(2)}, u32[]{:S(2)}) %collective-permute-start) | collective-permute-done | bytes 65568 | tf_op jit(solution)/shard_map/while/body/eval_jaxpr/ppermute | solution.py:14
  38.7 0.9 fusion.64
  39.7 3.4 %collective-permute-done = bf16[256,128]{1,0:T(8,128)(2,1)S(1)} collective-permute-done((bf16[256,128]{1,0:T(8,128)(2,1)S(1)}, bf16[256,128]{1,0:T(8,128)(2,1)S(1)}, u32[]{:S(2)}, u32[]{:S(2)}) %collective-permute-start) | collective-permute-done | bytes 65568 | tf_op jit(solution)/shard_map/while/body/eval_jaxpr/ppermute | solution.py:14
  45.2 0.9 fusion.64
  46.2 3.4 %collective-permute-done = bf16[256,128]{1,0:T(8,128)(2,1)S(1)} collective-permute-done((bf16[256,128]{1,0:T(8,128)(2,1)S(1)}, bf16[256,128]{1,0:T(8,128)(2,1)S(1)}, u32[]{:S(2)}, u32[]{:S(2)}) %collective-permute-start) | collective-permute-done | bytes 65568 | tf_op jit(solution)/shard_map/while/body/eval_jaxpr/ppermute | solution.py:14
  51.7 0.9 fusion.64
  52.7 3.4 %collective-permute-done = bf16[256,128]{1,0:T(8,128)(2,1)S(1)} collective-permute-done((bf16[256,128]{1,0:T(8,128)(2,1)S(1)}, bf16[256,128]{1,0:T(8,128)(2,1)S(1)}, u32[]{:S(2)}, u32[]{:S(2)}) %collective-permute-start) | collective-permute-done | bytes 65568 | tf_op jit(solution)/shard_map/while/body/eval_jaxpr/ppermute | solution.py:14
  58.2 0.9 fusion.64
  59.2 3.4 %collective-permute-done = bf16[256,128]{1,0:T(8,128)(2,1)S(1)} collective-permute-done((bf16[256,128]{1,0:T(8,128)(2,1)S(1)}, bf16[256,128]{1,0:T(8,128)(2,1)S(1)}, u32[]{:S(2)}, u32[]{:S(2)}) %collective-permute-start) | collective-permute-done | bytes 65568 | tf_op jit(solution)/shard_map/while/body/eval_jaxpr/ppermute | solution.py:14
  64.7 0.9 fusion.64
  65.7 3.4 %collective-permute-done = bf16[256,128]{1,0:T(8,128)(2,1)S(1)} collective-permute-done((bf16[256,128]{1,0:T(8,128)(2,1)S(1)}, bf16[256,128]{1,0:T(8,128)(2,1)S(1)}, u32[]{:S(2)}, u32[]{:S(2)}) %collective-permute-start) | collective-permute-done | bytes 65568 | tf_op jit(solution)/shard_map/while/body/eval_jaxpr/ppermute | solution.py:14
  71.3 0.9 fusion.64
  72.2 3.4 %collective-permute-done = bf16[256,128]{1,0:T(8,128)(2,1)S(1)} collective-permute-done((bf16[256,128]{1,0:T(8,128)(2,1)S(1)}, bf16[256,128]{1,0:T(8,128)(2,1)S(1)}, u32[]{:S(2)}, u32[]{:S(2)}) %collective-permute-start) | collective-permute-done | bytes 65568 | tf_op jit(solution)/shard_map/while/body/eval_jaxpr/ppermute | solution.py:14
  77.8 0.9 fusion.64
  78.7 3.4 %collective-permute-done = bf16[256,128]{1,0:T(8,128)(2,1)S(1)} collective-permute-done((bf16[256,128]{1,0:T(8,128)(2,1)S(1)}, bf16[256,128]{1,0:T(8,128)(2,1)S(1)}, u32[]{:S(2)}, u32[]{:S(2)}) %collective-permute-start) | collective-permute-done | bytes 65568 | tf_op jit(solution)/shard_map/while/body/eval_jaxpr/ppermute | solution.py:14
  84.3 0.9 fusion.64
  85.2 3.4 %collective-permute-done = bf16[256,128]{1,0:T(8,128)(2,1)S(1)} collective-permute-done((bf16[256,128]{1,0:T(8,128)(2,1)S(1)}, bf16[256,128]{1,0:T(8,128)(2,1)S(1)}, u32[]{:S(2)}, u32[]{:S(2)}) %collective-permute-start) | collective-permute-done | bytes 65568 | tf_op jit(solution)/shard_map/while/body/eval_jaxpr/ppermute | solution.py:14
  90.8 0.9 fusion.64
  91.8 3.4 %collective-permute-done = bf16[256,128]{1,0:T(8,128)(2,1)S(1)} collective-permute-done((bf16[256,128]{1,0:T(8,128)(2,1)S(1)}, bf16[256,128]{1,0:T(8,128)(2,1)S(1)}, u32[]{:S(2)}, u32[]{:S(2)}) %collective-permute-start) | collective-permute-done | bytes 65568 | tf_op jit(solution)/shard_map/while/body/eval_jaxpr/ppermute | solution.py:14
  97.3 0.9 fusion.64
  98.3 3.4 %collective-permute-done = bf16[256,128]{1,0:T(8,128)(2,1)S(1)} collective-permute-done((bf16[256,128]{1,0:T(8,128)(2,1)S(1)}, bf16[256,128]{1,0:T(8,128)(2,1)S(1)}, u32[]{:S(2)}, u32[]{:S(2)}) %collective-permute-start) | collective-permute-done | bytes 65568 | tf_op jit(solution)/shard_map/while/body/eval_jaxpr/ppermute | solution.py:14
  104.8 3.4 %collective-permute-done = bf16[256,128]{1,0:T(8,128)(2,1)S(1)} collective-permute-done((bf16[256,128]{1,0:T(8,128)(2,1)S(1)}, bf16[256,128]{1,0:T(8,128)(2,1)S(1)}, u32[]{:S(2)}, u32[]{:S(2)}) %collective-permute-start) | collective-permute-done | bytes 65568 | tf_op jit(solution)/shard_map/while/body/eval_jaxpr/ppermute | solution.py:14
  111.3 3.4 %collective-permute-done = bf16[256,128]{1,0:T(8,128)(2,1)S(1)} collective-permute-done((bf16[256,128]{1,0:T(8,128)(2,1)S(1)}, bf16[256,128]{1,0:T(8,128)(2,1)S(1)}, u32[]{:S(2)}, u32[]{:S(2)}) %collective-permute-start) | collective-permute-done | bytes 65568 | tf_op jit(solution)/shard_map/while/body/eval_jaxpr/ppermute | solution.py:14
  116.8 0.9 fusion.64
  117.8 3.4 %collective-permute-done = bf16[256,128]{1,0:T(8,128)(2,1)S(1)} collective-permute-done((bf16[256,128]{1,0:T(8,128)(2,1)S(1)}, bf16[256,128]{1,0:T(8,128)(2,1)S(1)}, u32[]{:S(2)}, u32[]{:S(2)}) %collective-permute-start) | collective-permute-done | bytes 65568 | tf_op jit(solution)/shard_map/while/body/eval_jaxpr/ppermute | solution.py:14
  123.3 0.9 fusion.64
  124.3 3.4 %collective-permute-done = bf16[256,128]{1,0:T(8,128)(2,1)S(1)} collective-permute-done((bf16[256,128]{1,0:T(8,128)(2,1)S(1)}, bf16[256,128]{1,0:T(8,128)(2,1)S(1)}, u32[]{:S(2)}, u32[]{:S(2)}) %collective-permute-start) | collective-permute-done | bytes 65568 | tf_op jit(solution)/shard_map/while/body/eval_jaxpr/ppermute | solution.py:14
  129.8 0.9 fusion.64
  130.8 3.4 %collective-permute-done = bf16[256,128]{1,0:T(8,128)(2,1)S(1)} collective-permute-done((bf16[256,128]{1,0:T(8,128)(2,1)S(1)}, bf16[256,128]{1,0:T(8,128)(2,1)S(1)}, u32[]{:S(2)}, u32[]{:S(2)}) %collective-permute-start) | collective-permute-done | bytes 65568 | tf_op jit(solution)/shard_map/while/body/eval_jaxpr/ppermute | solution.py:14
  136.3 0.9 fusion.64
  137.3 3.4 %collective-permute-done = bf16[256,128]{1,0:T(8,128)(2,1)S(1)} collective-permute-done((bf16[256,128]{1,0:T(8,128)(2,1)S(1)}, bf16[256,128]{1,0:T(8,128)(2,1)S(1)}, u32[]{:S(2)}, u32[]{:S(2)}) %collective-permute-start) | collective-permute-done | bytes 65568 | tf_op jit(solution)/shard_map/while/body/eval_jaxpr/ppermute | solution.py:14
  142.9 0.9 fusion.64
  143.8 3.4 %collective-permute-done = bf16[256,128]{1,0:T(8,128)(2,1)S(1)} collective-permute-done((bf16[256,128]{1,0:T(8,128)(2,1)S(1)}, bf16[256,128]{1,0:T(8,128)(2,1)S(1)}, u32[]{:S(2)}, u32[]{:S(2)}) %collective-permute-start) | collective-permute-done | bytes 65568 | tf_op jit(solution)/shard_map/while/body/eval_jaxpr/ppermute | solution.py:14
  149.4 0.9 fusion.64
  150.3 3.4 %collective-permute-done = bf16[256,128]{1,0:T(8,128)(2,1)S(1)} collective-permute-done((bf16[256,128]{1,0:T(8,128)(2,1)S(1)}, bf16[256,128]{1,0:T(8,128)(2,1)S(1)}, u32[]{:S(2)}, u32[]{:S(2)}) %collective-permute-start) | collective-permute-done | bytes 65568 | tf_op jit(solution)/shard_map/while/body/eval_jaxpr/ppermute | solution.py:14
  155.9 0.9 fusion.64
  156.8 3.4 %collective-permute-done = bf16[256,128]{1,0:T(8,128)(2,1)S(1)} collective-permute-done((bf16[256,128]{1,0:T(8,128)(2,1)S(1)}, bf16[256,128]{1,0:T(8,128)(2,1)S(1)}, u32[]{:S(2)}, u32[]{:S(2)}) %collective-permute-start) | collective-permute-done | bytes 65568 | tf_op jit(solution)/shard_map/while/body/eval_jaxpr/ppermute | solution.py:14
  162.4 0.9 fusion.64
  163.3 3.4 %collective-permute-done = bf16[256,128]{1,0:T(8,128)(2,1)S(1)} collective-permute-done((bf16[256,128]{1,0:T(8,128)(2,1)S(1)}, bf16[256,128]{1,0:T(8,128)(2,1)S(1)}, u32[]{:S(2)}, u32[]{:S(2)}) %collective-permute-start) | collective-permute-done | bytes 65568 | tf_op jit(solution)/shard_map/while/body/eval_jaxpr/ppermute | solution.py:14
  168.9 0.9 fusion.64
  169.9 3.4 %collective-permute-done = bf16[256,128]{1,0:T(8,128)(2,1)S(1)} collective-permute-done((bf16[256,128]{1,0:T(8,128)(2,1)S(1)}, bf16[256,128]{1,0:T(8,128)(2,1)S(1)}, u32[]{:S(2)}, u32[]{:S(2)}) %collective-permute-start) | collective-permute-done | bytes 65568 | tf_op jit(solution)/shard_map/while/body/eval_jaxpr/ppermute | solution.py:14
  175.4 0.9 fusion.64
  176.4 3.4 %collective-permute-done = bf16[256,128]{1,0:T(8,128)(2,1)S(1)} collective-permute-done((bf16[256,128]{1,0:T(8,128)(2,1)S(1)}, bf16[256,128]{1,0:T(8,128)(2,1)S(1)}, u32[]{:S(2)}, u32[]{:S(2)}) %collective-permute-start) | collective-permute-done | bytes 65568 | tf_op jit(solution)/shard_map/while/body/eval_jaxpr/ppermute | solution.py:14
  181.9 0.9 fusion.64
  182.9 3.4 %collective-permute-done = bf16[256,128]{1,0:T(8,128)(2,1)S(1)} collective-permute-done((bf16[256,128]{1,0:T(8,128)(2,1)S(1)}, bf16[256,128]{1,0:T(8,128)(2,1)S(1)}, u32[]{:S(2)}, u32[]{:S(2)}) %collective-permute-start) | collective-permute-done | bytes 65568 | tf_op jit(solution)/shard_map/while/body/eval_jaxpr/ppermute | solution.py:14
  188.4 0.9 fusion.64
  189.4 3.4 %collective-permute-done = bf16[256,128]{1,0:T(8,128)(2,1)S(1)} collective-permute-done((bf16[256,128]{1,0:T(8,128)(2,1)S(1)}, bf16[256,128]{1,0:T(8,128)(2,1)S(1)}, u32[]{:S(2)}, u32[]{:S(2)}) %collective-permute-start) | collective-permute-done | bytes 65568 | tf_op jit(solution)/shard_map/while/body/eval_jaxpr/ppermute | solution.py:14
  194.9 0.9 fusion.64
  195.9 3.4 %collective-permute-done = bf16[256,128]{1,0:T(8,128)(2,1)S(1)} collective-permute-done((bf16[256,128]{1,0:T(8,128)(2,1)S(1)}, bf16[256,128]{1,0:T(8,128)(2,1)S(1)}, u32[]{:S(2)}, u32[]{:S(2)}) %collective-permute-start) | collective-permute-done | bytes 65568 | tf_op jit(solution)/shard_map/while/body/eval_jaxpr/ppermute | solution.py:14
  202.4 3.4 %collective-permute-done = bf16[256,128]{1,0:T(8,128)(2,1)S(1)} collective-permute-done((bf16[256,128]{1,0:T(8,128)(2,1)S(1)}, bf16[256,128]{1,0:T(8,128)(2,1)S(1)}, u32[]{:S(2)}, u32[]{:S(2)}) %collective-permute-start) | collective-permute-done | bytes 65568 | tf_op jit(solution)/shard_map/while/body/eval_jaxpr/ppermute | solution.py:14
  207.5 1.2 fusion.29
  209.2 12.9 %all_to_all.16 = bf16[8,32,1024]{2,1,0:T(8,128)(2,1)S(1)} all-to-all(bf16[8,32,1024]{2,1,0:T(8,128)(2,1)S(1)} %convert_element_type.46), channel_id=1, replica_groups=mesh['ctx'=32,'head'=8] {'head'}, dimensions={0} | all-to-all | bytes 1048576 | tf_op jit(solution)/shard_map/all_to_all | solution.py:95
  (495 shorter events, 71.1 us)
Async XLA Ops:
  0.0 2.9 %copy-start.1 = (bf16[256,128]{1,0:T(8,128)(2,1)S(1)}, bf16[256,128]{1,0:T(8,128)(2,1)}, u32[]{:S(2)}) copy-start(bf16[256,128]{1,0:T(8,128)(2,1)} %param.9) | copy-start | bytes 196612
  2.9 203.6 %copy-start.2 = (bf16[256,1024]{1,0:T(8,128)(2,1)S(1)}, bf16[256,1024]{1,0:T(8,128)(2,1)}, u32[]{:S(2)}) copy-start(bf16[256,1024]{1,0:T(8,128)(2,1)} %param.7) | copy-start | bytes 1572868
  2.9 7.6 %collective-permute-start = (bf16[256,128]{1,0:T(8,128)(2,1)S(1)}, bf16[256,128]{1,0:T(8,128)(2,1)S(1)}, u32[]{:S(2)}, u32[]{:S(2)}) collective-permute-start(bf16[256,128]{1,0:T(8,128)(2,1)S(1)} %copy.53), channel_id=1, source_target_pairs={{248,0},{0,8},{8,16},{16,24},{24,32},{32,40},{40,48},{48,56},{56,6... | collective-permute-start | bytes 196616 | tf_op jit(solution)/shard_map/while/body/eval_jaxpr/ppermute | solution.py:14
  3.0 8.2 %collective-permute-start.1 = (bf16[256,128]{1,0:T(8,128)(2,1)S(1)}, bf16[256,128]{1,0:T(8,128)(2,1)S(1)}, u32[]{:S(2)}, u32[]{:S(2)}) collective-permute-start(bf16[256,128]{1,0:T(8,128)(2,1)S(1)} %copy.54), channel_id=1, source_target_pairs={{248,0},{0,8},{8,16},{16,24},{24,32},{32,40},{40,48},{48,56},{56,6... | collective-permute-start | bytes 196616 | tf_op jit(solution)/shard_map/while/body/eval_jaxpr/ppermute | solution.py:14
  11.2 5.8 %collective-permute-start = (bf16[256,128]{1,0:T(8,128)(2,1)S(1)}, bf16[256,128]{1,0:T(8,128)(2,1)S(1)}, u32[]{:S(2)}, u32[]{:S(2)}) collective-permute-start(bf16[256,128]{1,0:T(8,128)(2,1)S(1)} %copy.53), channel_id=1, source_target_pairs={{248,0},{0,8},{8,16},{16,24},{24,32},{32,40},{40,48},{48,56},{56,6... | collective-permute-start | bytes 196616 | tf_op jit(solution)/shard_map/while/body/eval_jaxpr/ppermute | solution.py:14
  11.3 6.5 %collective-permute-start.1 = (bf16[256,128]{1,0:T(8,128)(2,1)S(1)}, bf16[256,128]{1,0:T(8,128)(2,1)S(1)}, u32[]{:S(2)}, u32[]{:S(2)}) collective-permute-start(bf16[256,128]{1,0:T(8,128)(2,1)S(1)} %copy.54), channel_id=1, source_target_pairs={{248,0},{0,8},{8,16},{16,24},{24,32},{32,40},{40,48},{48,56},{56,6... | collective-permute-start | bytes 196616 | tf_op jit(solution)/shard_map/while/body/eval_jaxpr/ppermute | solution.py:14
  17.7 5.8 %collective-permute-start = (bf16[256,128]{1,0:T(8,128)(2,1)S(1)}, bf16[256,128]{1,0:T(8,128)(2,1)S(1)}, u32[]{:S(2)}, u32[]{:S(2)}) collective-permute-start(bf16[256,128]{1,0:T(8,128)(2,1)S(1)} %copy.53), channel_id=1, source_target_pairs={{248,0},{0,8},{8,16},{16,24},{24,32},{32,40},{40,48},{48,56},{56,6... | collective-permute-start | bytes 196616 | tf_op jit(solution)/shard_map/while/body/eval_jaxpr/ppermute | solution.py:14
  17.8 6.5 %collective-permute-start.1 = (bf16[256,128]{1,0:T(8,128)(2,1)S(1)}, bf16[256,128]{1,0:T(8,128)(2,1)S(1)}, u32[]{:S(2)}, u32[]{:S(2)}) collective-permute-start(bf16[256,128]{1,0:T(8,128)(2,1)S(1)} %copy.54), channel_id=1, source_target_pairs={{248,0},{0,8},{8,16},{16,24},{24,32},{32,40},{40,48},{48,56},{56,6... | collective-permute-start | bytes 196616 | tf_op jit(solution)/shard_map/while/body/eval_jaxpr/ppermute | solution.py:14
  24.2 5.8 %collective-permute-start = (bf16[256,128]{1,0:T(8,128)(2,1)S(1)}, bf16[256,128]{1,0:T(8,128)(2,1)S(1)}, u32[]{:S(2)}, u32[]{:S(2)}) collective-permute-start(bf16[256,128]{1,0:T(8,128)(2,1)S(1)} %copy.53), channel_id=1, source_target_pairs={{248,0},{0,8},{8,16},{16,24},{24,32},{32,40},{40,48},{48,56},{56,6... | collective-permute-start | bytes 196616 | tf_op jit(solution)/shard_map/while/body/eval_jaxpr/ppermute | solution.py:14
  24.3 6.5 %collective-permute-start.1 = (bf16[256,128]{1,0:T(8,128)(2,1)S(1)}, bf16[256,128]{1,0:T(8,128)(2,1)S(1)}, u32[]{:S(2)}, u32[]{:S(2)}) collective-permute-start(bf16[256,128]{1,0:T(8,128)(2,1)S(1)} %copy.54), channel_id=1, source_target_pairs={{248,0},{0,8},{8,16},{16,24},{24,32},{32,40},{40,48},{48,56},{56,6... | collective-permute-start | bytes 196616 | tf_op jit(solution)/shard_map/while/body/eval_jaxpr/ppermute | solution.py:14
  30.8 5.8 %collective-permute-start = (bf16[256,128]{1,0:T(8,128)(2,1)S(1)}, bf16[256,128]{1,0:T(8,128)(2,1)S(1)}, u32[]{:S(2)}, u32[]{:S(2)}) collective-permute-start(bf16[256,128]{1,0:T(8,128)(2,1)S(1)} %copy.53), channel_id=1, source_target_pairs={{248,0},{0,8},{8,16},{16,24},{24,32},{32,40},{40,48},{48,56},{56,6... | collective-permute-start | bytes 196616 | tf_op jit(solution)/shard_map/while/body/eval_jaxpr/ppermute | solution.py:14
  30.8 6.5 %collective-permute-start.1 = (bf16[256,128]{1,0:T(8,128)(2,1)S(1)}, bf16[256,128]{1,0:T(8,128)(2,1)S(1)}, u32[]{:S(2)}, u32[]{:S(2)}) collective-permute-start(bf16[256,128]{1,0:T(8,128)(2,1)S(1)} %copy.54), channel_id=1, source_target_pairs={{248,0},{0,8},{8,16},{16,24},{24,32},{32,40},{40,48},{48,56},{56,6... | collective-permute-start | bytes 196616 | tf_op jit(solution)/shard_map/while/body/eval_jaxpr/ppermute | solution.py:14
  37.3 5.8 %collective-permute-start = (bf16[256,128]{1,0:T(8,128)(2,1)S(1)}, bf16[256,128]{1,0:T(8,128)(2,1)S(1)}, u32[]{:S(2)}, u32[]{:S(2)}) collective-permute-start(bf16[256,128]{1,0:T(8,128)(2,1)S(1)} %copy.53), channel_id=1, source_target_pairs={{248,0},{0,8},{8,16},{16,24},{24,32},{32,40},{40,48},{48,56},{56,6... | collective-permute-start | bytes 196616 | tf_op jit(solution)/shard_map/while/body/eval_jaxpr/ppermute | solution.py:14
  37.3 6.5 %collective-permute-start.1 = (bf16[256,128]{1,0:T(8,128)(2,1)S(1)}, bf16[256,128]{1,0:T(8,128)(2,1)S(1)}, u32[]{:S(2)}, u32[]{:S(2)}) collective-permute-start(bf16[256,128]{1,0:T(8,128)(2,1)S(1)} %copy.54), channel_id=1, source_target_pairs={{248,0},{0,8},{8,16},{16,24},{24,32},{32,40},{40,48},{48,56},{56,6... | collective-permute-start | bytes 196616 | tf_op jit(solution)/shard_map/while/body/eval_jaxpr/ppermute | solution.py:14
  43.8 5.8 %collective-permute-start = (bf16[256,128]{1,0:T(8,128)(2,1)S(1)}, bf16[256,128]{1,0:T(8,128)(2,1)S(1)}, u32[]{:S(2)}, u32[]{:S(2)}) collective-permute-start(bf16[256,128]{1,0:T(8,128)(2,1)S(1)} %copy.53), channel_id=1, source_target_pairs={{248,0},{0,8},{8,16},{16,24},{24,32},{32,40},{40,48},{48,56},{56,6... | collective-permute-start | bytes 196616 | tf_op jit(solution)/shard_map/while/body/eval_jaxpr/ppermute | solution.py:14
  43.8 6.5 %collective-permute-start.1 = (bf16[256,128]{1,0:T(8,128)(2,1)S(1)}, bf16[256,128]{1,0:T(8,128)(2,1)S(1)}, u32[]{:S(2)}, u32[]{:S(2)}) collective-permute-start(bf16[256,128]{1,0:T(8,128)(2,1)S(1)} %copy.54), channel_id=1, source_target_pairs={{248,0},{0,8},{8,16},{16,24},{24,32},{32,40},{40,48},{48,56},{56,6... | collective-permute-start | bytes 196616 | tf_op jit(solution)/shard_map/while/body/eval_jaxpr/ppermute | solution.py:14
  50.3 5.8 %collective-permute-start = (bf16[256,128]{1,0:T(8,128)(2,1)S(1)}, bf16[256,128]{1,0:T(8,128)(2,1)S(1)}, u32[]{:S(2)}, u32[]{:S(2)}) collective-permute-start(bf16[256,128]{1,0:T(8,128)(2,1)S(1)} %copy.53), channel_id=1, source_target_pairs={{248,0},{0,8},{8,16},{16,24},{24,32},{32,40},{40,48},{48,56},{56,6... | collective-permute-start | bytes 196616 | tf_op jit(solution)/shard_map/while/body/eval_jaxpr/ppermute | solution.py:14
  50.3 6.5 %collective-permute-start.1 = (bf16[256,128]{1,0:T(8,128)(2,1)S(1)}, bf16[256,128]{1,0:T(8,128)(2,1)S(1)}, u32[]{:S(2)}, u32[]{:S(2)}) collective-permute-start(bf16[256,128]{1,0:T(8,128)(2,1)S(1)} %copy.54), channel_id=1, source_target_pairs={{248,0},{0,8},{8,16},{16,24},{24,32},{32,40},{40,48},{48,56},{56,6... | collective-permute-start | bytes 196616 | tf_op jit(solution)/shard_map/while/body/eval_jaxpr/ppermute | solution.py:14
  56.8 5.8 %collective-permute-start = (bf16[256,128]{1,0:T(8,128)(2,1)S(1)}, bf16[256,128]{1,0:T(8,128)(2,1)S(1)}, u32[]{:S(2)}, u32[]{:S(2)}) collective-permute-start(bf16[256,128]{1,0:T(8,128)(2,1)S(1)} %copy.53), channel_id=1, source_target_pairs={{248,0},{0,8},{8,16},{16,24},{24,32},{32,40},{40,48},{48,56},{56,6... | collective-permute-start | bytes 196616 | tf_op jit(solution)/shard_map/while/body/eval_jaxpr/ppermute | solution.py:14
  56.8 6.5 %collective-permute-start.1 = (bf16[256,128]{1,0:T(8,128)(2,1)S(1)}, bf16[256,128]{1,0:T(8,128)(2,1)S(1)}, u32[]{:S(2)}, u32[]{:S(2)}) collective-permute-start(bf16[256,128]{1,0:T(8,128)(2,1)S(1)} %copy.54), channel_id=1, source_target_pairs={{248,0},{0,8},{8,16},{16,24},{24,32},{32,40},{40,48},{48,56},{56,6... | collective-permute-start | bytes 196616 | tf_op jit(solution)/shard_map/while/body/eval_jaxpr/ppermute | solution.py:14
  63.3 5.8 %collective-permute-start = (bf16[256,128]{1,0:T(8,128)(2,1)S(1)}, bf16[256,128]{1,0:T(8,128)(2,1)S(1)}, u32[]{:S(2)}, u32[]{:S(2)}) collective-permute-start(bf16[256,128]{1,0:T(8,128)(2,1)S(1)} %copy.53), channel_id=1, source_target_pairs={{248,0},{0,8},{8,16},{16,24},{24,32},{32,40},{40,48},{48,56},{56,6... | collective-permute-start | bytes 196616 | tf_op jit(solution)/shard_map/while/body/eval_jaxpr/ppermute | solution.py:14
  63.3 6.5 %collective-permute-start.1 = (bf16[256,128]{1,0:T(8,128)(2,1)S(1)}, bf16[256,128]{1,0:T(8,128)(2,1)S(1)}, u32[]{:S(2)}, u32[]{:S(2)}) collective-permute-start(bf16[256,128]{1,0:T(8,128)(2,1)S(1)} %copy.54), channel_id=1, source_target_pairs={{248,0},{0,8},{8,16},{16,24},{24,32},{32,40},{40,48},{48,56},{56,6... | collective-permute-start | bytes 196616 | tf_op jit(solution)/shard_map/while/body/eval_jaxpr/ppermute | solution.py:14
  69.8 5.8 %collective-permute-start = (bf16[256,128]{1,0:T(8,128)(2,1)S(1)}, bf16[256,128]{1,0:T(8,128)(2,1)S(1)}, u32[]{:S(2)}, u32[]{:S(2)}) collective-permute-start(bf16[256,128]{1,0:T(8,128)(2,1)S(1)} %copy.53), channel_id=1, source_target_pairs={{248,0},{0,8},{8,16},{16,24},{24,32},{32,40},{40,48},{48,56},{56,6... | collective-permute-start | bytes 196616 | tf_op jit(solution)/shard_map/while/body/eval_jaxpr/ppermute | solution.py:14
  69.8 6.5 %collective-permute-start.1 = (bf16[256,128]{1,0:T(8,128)(2,1)S(1)}, bf16[256,128]{1,0:T(8,128)(2,1)S(1)}, u32[]{:S(2)}, u32[]{:S(2)}) collective-permute-start(bf16[256,128]{1,0:T(8,128)(2,1)S(1)} %copy.54), channel_id=1, source_target_pairs={{248,0},{0,8},{8,16},{16,24},{24,32},{32,40},{40,48},{48,56},{56,6... | collective-permute-start | bytes 196616 | tf_op jit(solution)/shard_map/while/body/eval_jaxpr/ppermute | solution.py:14
  76.3 5.8 %collective-permute-start = (bf16[256,128]{1,0:T(8,128)(2,1)S(1)}, bf16[256,128]{1,0:T(8,128)(2,1)S(1)}, u32[]{:S(2)}, u32[]{:S(2)}) collective-permute-start(bf16[256,128]{1,0:T(8,128)(2,1)S(1)} %copy.53), channel_id=1, source_target_pairs={{248,0},{0,8},{8,16},{16,24},{24,32},{32,40},{40,48},{48,56},{56,6... | collective-permute-start | bytes 196616 | tf_op jit(solution)/shard_map/while/body/eval_jaxpr/ppermute | solution.py:14
  76.3 6.5 %collective-permute-start.1 = (bf16[256,128]{1,0:T(8,128)(2,1)S(1)}, bf16[256,128]{1,0:T(8,128)(2,1)S(1)}, u32[]{:S(2)}, u32[]{:S(2)}) collective-permute-start(bf16[256,128]{1,0:T(8,128)(2,1)S(1)} %copy.54), channel_id=1, source_target_pairs={{248,0},{0,8},{8,16},{16,24},{24,32},{32,40},{40,48},{48,56},{56,6... | collective-permute-start | bytes 196616 | tf_op jit(solution)/shard_map/while/body/eval_jaxpr/ppermute | solution.py:14
  82.8 5.8 %collective-permute-start = (bf16[256,128]{1,0:T(8,128)(2,1)S(1)}, bf16[256,128]{1,0:T(8,128)(2,1)S(1)}, u32[]{:S(2)}, u32[]{:S(2)}) collective-permute-start(bf16[256,128]{1,0:T(8,128)(2,1)S(1)} %copy.53), channel_id=1, source_target_pairs={{248,0},{0,8},{8,16},{16,24},{24,32},{32,40},{40,48},{48,56},{56,6... | collective-permute-start | bytes 196616 | tf_op jit(solution)/shard_map/while/body/eval_jaxpr/ppermute | solution.py:14
  82.9 6.5 %collective-permute-start.1 = (bf16[256,128]{1,0:T(8,128)(2,1)S(1)}, bf16[256,128]{1,0:T(8,128)(2,1)S(1)}, u32[]{:S(2)}, u32[]{:S(2)}) collective-permute-start(bf16[256,128]{1,0:T(8,128)(2,1)S(1)} %copy.54), channel_id=1, source_target_pairs={{248,0},{0,8},{8,16},{16,24},{24,32},{32,40},{40,48},{48,56},{56,6... | collective-permute-start | bytes 196616 | tf_op jit(solution)/shard_map/while/body/eval_jaxpr/ppermute | solution.py:14
  89.3 5.8 %collective-permute-start = (bf16[256,128]{1,0:T(8,128)(2,1)S(1)}, bf16[256,128]{1,0:T(8,128)(2,1)S(1)}, u32[]{:S(2)}, u32[]{:S(2)}) collective-permute-start(bf16[256,128]{1,0:T(8,128)(2,1)S(1)} %copy.53), channel_id=1, source_target_pairs={{248,0},{0,8},{8,16},{16,24},{24,32},{32,40},{40,48},{48,56},{56,6... | collective-permute-start | bytes 196616 | tf_op jit(solution)/shard_map/while/body/eval_jaxpr/ppermute | solution.py:14
  89.4 6.5 %collective-permute-start.1 = (bf16[256,128]{1,0:T(8,128)(2,1)S(1)}, bf16[256,128]{1,0:T(8,128)(2,1)S(1)}, u32[]{:S(2)}, u32[]{:S(2)}) collective-permute-start(bf16[256,128]{1,0:T(8,128)(2,1)S(1)} %copy.54), channel_id=1, source_target_pairs={{248,0},{0,8},{8,16},{16,24},{24,32},{32,40},{40,48},{48,56},{56,6... | collective-permute-start | bytes 196616 | tf_op jit(solution)/shard_map/while/body/eval_jaxpr/ppermute | solution.py:14
  95.8 5.8 %collective-permute-start = (bf16[256,128]{1,0:T(8,128)(2,1)S(1)}, bf16[256,128]{1,0:T(8,128)(2,1)S(1)}, u32[]{:S(2)}, u32[]{:S(2)}) collective-permute-start(bf16[256,128]{1,0:T(8,128)(2,1)S(1)} %copy.53), channel_id=1, source_target_pairs={{248,0},{0,8},{8,16},{16,24},{24,32},{32,40},{40,48},{48,56},{56,6... | collective-permute-start | bytes 196616 | tf_op jit(solution)/shard_map/while/body/eval_jaxpr/ppermute | solution.py:14
  95.9 6.5 %collective-permute-start.1 = (bf16[256,128]{1,0:T(8,128)(2,1)S(1)}, bf16[256,128]{1,0:T(8,128)(2,1)S(1)}, u32[]{:S(2)}, u32[]{:S(2)}) collective-permute-start(bf16[256,128]{1,0:T(8,128)(2,1)S(1)} %copy.54), channel_id=1, source_target_pairs={{248,0},{0,8},{8,16},{16,24},{24,32},{32,40},{40,48},{48,56},{56,6... | collective-permute-start | bytes 196616 | tf_op jit(solution)/shard_map/while/body/eval_jaxpr/ppermute | solution.py:14
  102.4 5.8 %collective-permute-start = (bf16[256,128]{1,0:T(8,128)(2,1)S(1)}, bf16[256,128]{1,0:T(8,128)(2,1)S(1)}, u32[]{:S(2)}, u32[]{:S(2)}) collective-permute-start(bf16[256,128]{1,0:T(8,128)(2,1)S(1)} %copy.53), channel_id=1, source_target_pairs={{248,0},{0,8},{8,16},{16,24},{24,32},{32,40},{40,48},{48,56},{56,6... | collective-permute-start | bytes 196616 | tf_op jit(solution)/shard_map/while/body/eval_jaxpr/ppermute | solution.py:14
  102.4 6.5 %collective-permute-start.1 = (bf16[256,128]{1,0:T(8,128)(2,1)S(1)}, bf16[256,128]{1,0:T(8,128)(2,1)S(1)}, u32[]{:S(2)}, u32[]{:S(2)}) collective-permute-start(bf16[256,128]{1,0:T(8,128)(2,1)S(1)} %copy.54), channel_id=1, source_target_pairs={{248,0},{0,8},{8,16},{16,24},{24,32},{32,40},{40,48},{48,56},{56,6... | collective-permute-start | bytes 196616 | tf_op jit(solution)/shard_map/while/body/eval_jaxpr/ppermute | solution.py:14
  108.9 5.8 %collective-permute-start = (bf16[256,128]{1,0:T(8,128)(2,1)S(1)}, bf16[256,128]{1,0:T(8,128)(2,1)S(1)}, u32[]{:S(2)}, u32[]{:S(2)}) collective-permute-start(bf16[256,128]{1,0:T(8,128)(2,1)S(1)} %copy.53), channel_id=1, source_target_pairs={{248,0},{0,8},{8,16},{16,24},{24,32},{32,40},{40,48},{48,56},{56,6... | collective-permute-start | bytes 196616 | tf_op jit(solution)/shard_map/while/body/eval_jaxpr/ppermute | solution.py:14
  108.9 6.5 %collective-permute-start.1 = (bf16[256,128]{1,0:T(8,128)(2,1)S(1)}, bf16[256,128]{1,0:T(8,128)(2,1)S(1)}, u32[]{:S(2)}, u32[]{:S(2)}) collective-permute-start(bf16[256,128]{1,0:T(8,128)(2,1)S(1)} %copy.54), channel_id=1, source_target_pairs={{248,0},{0,8},{8,16},{16,24},{24,32},{32,40},{40,48},{48,56},{56,6... | collective-permute-start | bytes 196616 | tf_op jit(solution)/shard_map/while/body/eval_jaxpr/ppermute | solution.py:14
  115.4 5.8 %collective-permute-start = (bf16[256,128]{1,0:T(8,128)(2,1)S(1)}, bf16[256,128]{1,0:T(8,128)(2,1)S(1)}, u32[]{:S(2)}, u32[]{:S(2)}) collective-permute-start(bf16[256,128]{1,0:T(8,128)(2,1)S(1)} %copy.53), channel_id=1, source_target_pairs={{248,0},{0,8},{8,16},{16,24},{24,32},{32,40},{40,48},{48,56},{56,6... | collective-permute-start | bytes 196616 | tf_op jit(solution)/shard_map/while/body/eval_jaxpr/ppermute | solution.py:14
  115.4 6.5 %collective-permute-start.1 = (bf16[256,128]{1,0:T(8,128)(2,1)S(1)}, bf16[256,128]{1,0:T(8,128)(2,1)S(1)}, u32[]{:S(2)}, u32[]{:S(2)}) collective-permute-start(bf16[256,128]{1,0:T(8,128)(2,1)S(1)} %copy.54), channel_id=1, source_target_pairs={{248,0},{0,8},{8,16},{16,24},{24,32},{32,40},{40,48},{48,56},{56,6... | collective-permute-start | bytes 196616 | tf_op jit(solution)/shard_map/while/body/eval_jaxpr/ppermute | solution.py:14
  121.9 5.8 %collective-permute-start = (bf16[256,128]{1,0:T(8,128)(2,1)S(1)}, bf16[256,128]{1,0:T(8,128)(2,1)S(1)}, u32[]{:S(2)}, u32[]{:S(2)}) collective-permute-start(bf16[256,128]{1,0:T(8,128)(2,1)S(1)} %copy.53), channel_id=1, source_target_pairs={{248,0},{0,8},{8,16},{16,24},{24,32},{32,40},{40,48},{48,56},{56,6... | collective-permute-start | bytes 196616 | tf_op jit(solution)/shard_map/while/body/eval_jaxpr/ppermute | solution.py:14
  121.9 6.5 %collective-permute-start.1 = (bf16[256,128]{1,0:T(8,128)(2,1)S(1)}, bf16[256,128]{1,0:T(8,128)(2,1)S(1)}, u32[]{:S(2)}, u32[]{:S(2)}) collective-permute-start(bf16[256,128]{1,0:T(8,128)(2,1)S(1)} %copy.54), channel_id=1, source_target_pairs={{248,0},{0,8},{8,16},{16,24},{24,32},{32,40},{40,48},{48,56},{56,6... | collective-permute-start | bytes 196616 | tf_op jit(solution)/shard_map/while/body/eval_jaxpr/ppermute | solution.py:14
  128.4 5.8 %collective-permute-start = (bf16[256,128]{1,0:T(8,128)(2,1)S(1)}, bf16[256,128]{1,0:T(8,128)(2,1)S(1)}, u32[]{:S(2)}, u32[]{:S(2)}) collective-permute-start(bf16[256,128]{1,0:T(8,128)(2,1)S(1)} %copy.53), channel_id=1, source_target_pairs={{248,0},{0,8},{8,16},{16,24},{24,32},{32,40},{40,48},{48,56},{56,6... | collective-permute-start | bytes 196616 | tf_op jit(solution)/shard_map/while/body/eval_jaxpr/ppermute | solution.py:14
  128.4 6.5 %collective-permute-start.1 = (bf16[256,128]{1,0:T(8,128)(2,1)S(1)}, bf16[256,128]{1,0:T(8,128)(2,1)S(1)}, u32[]{:S(2)}, u32[]{:S(2)}) collective-permute-start(bf16[256,128]{1,0:T(8,128)(2,1)S(1)} %copy.54), channel_id=1, source_target_pairs={{248,0},{0,8},{8,16},{16,24},{24,32},{32,40},{40,48},{48,56},{56,6... | collective-permute-start | bytes 196616 | tf_op jit(solution)/shard_map/while/body/eval_jaxpr/ppermute | solution.py:14
  134.9 5.8 %collective-permute-start = (bf16[256,128]{1,0:T(8,128)(2,1)S(1)}, bf16[256,128]{1,0:T(8,128)(2,1)S(1)}, u32[]{:S(2)}, u32[]{:S(2)}) collective-permute-start(bf16[256,128]{1,0:T(8,128)(2,1)S(1)} %copy.53), channel_id=1, source_target_pairs={{248,0},{0,8},{8,16},{16,24},{24,32},{32,40},{40,48},{48,56},{56,6... | collective-permute-start | bytes 196616 | tf_op jit(solution)/shard_map/while/body/eval_jaxpr/ppermute | solution.py:14
  134.9 6.5 %collective-permute-start.1 = (bf16[256,128]{1,0:T(8,128)(2,1)S(1)}, bf16[256,128]{1,0:T(8,128)(2,1)S(1)}, u32[]{:S(2)}, u32[]{:S(2)}) collective-permute-start(bf16[256,128]{1,0:T(8,128)(2,1)S(1)} %copy.54), channel_id=1, source_target_pairs={{248,0},{0,8},{8,16},{16,24},{24,32},{32,40},{40,48},{48,56},{56,6... | collective-permute-start | bytes 196616 | tf_op jit(solution)/shard_map/while/body/eval_jaxpr/ppermute | solution.py:14
  141.4 5.8 %collective-permute-start = (bf16[256,128]{1,0:T(8,128)(2,1)S(1)}, bf16[256,128]{1,0:T(8,128)(2,1)S(1)}, u32[]{:S(2)}, u32[]{:S(2)}) collective-permute-start(bf16[256,128]{1,0:T(8,128)(2,1)S(1)} %copy.53), channel_id=1, source_target_pairs={{248,0},{0,8},{8,16},{16,24},{24,32},{32,40},{40,48},{48,56},{56,6... | collective-permute-start | bytes 196616 | tf_op jit(solution)/shard_map/while/body/eval_jaxpr/ppermute | solution.py:14
  141.4 6.5 %collective-permute-start.1 = (bf16[256,128]{1,0:T(8,128)(2,1)S(1)}, bf16[256,128]{1,0:T(8,128)(2,1)S(1)}, u32[]{:S(2)}, u32[]{:S(2)}) collective-permute-start(bf16[256,128]{1,0:T(8,128)(2,1)S(1)} %copy.54), channel_id=1, source_target_pairs={{248,0},{0,8},{8,16},{16,24},{24,32},{32,40},{40,48},{48,56},{56,6... | collective-permute-start | bytes 196616 | tf_op jit(solution)/shard_map/while/body/eval_jaxpr/ppermute | solution.py:14
  147.9 5.8 %collective-permute-start = (bf16[256,128]{1,0:T(8,128)(2,1)S(1)}, bf16[256,128]{1,0:T(8,128)(2,1)S(1)}, u32[]{:S(2)}, u32[]{:S(2)}) collective-permute-start(bf16[256,128]{1,0:T(8,128)(2,1)S(1)} %copy.53), channel_id=1, source_target_pairs={{248,0},{0,8},{8,16},{16,24},{24,32},{32,40},{40,48},{48,56},{56,6... | collective-permute-start | bytes 196616 | tf_op jit(solution)/shard_map/while/body/eval_jaxpr/ppermute | solution.py:14
  147.9 6.5 %collective-permute-start.1 = (bf16[256,128]{1,0:T(8,128)(2,1)S(1)}, bf16[256,128]{1,0:T(8,128)(2,1)S(1)}, u32[]{:S(2)}, u32[]{:S(2)}) collective-permute-start(bf16[256,128]{1,0:T(8,128)(2,1)S(1)} %copy.54), channel_id=1, source_target_pairs={{248,0},{0,8},{8,16},{16,24},{24,32},{32,40},{40,48},{48,56},{56,6... | collective-permute-start | bytes 196616 | tf_op jit(solution)/shard_map/while/body/eval_jaxpr/ppermute | solution.py:14
  154.4 5.8 %collective-permute-start = (bf16[256,128]{1,0:T(8,128)(2,1)S(1)}, bf16[256,128]{1,0:T(8,128)(2,1)S(1)}, u32[]{:S(2)}, u32[]{:S(2)}) collective-permute-start(bf16[256,128]{1,0:T(8,128)(2,1)S(1)} %copy.53), channel_id=1, source_target_pairs={{248,0},{0,8},{8,16},{16,24},{24,32},{32,40},{40,48},{48,56},{56,6... | collective-permute-start | bytes 196616 | tf_op jit(solution)/shard_map/while/body/eval_jaxpr/ppermute | solution.py:14
  154.5 6.5 %collective-permute-start.1 = (bf16[256,128]{1,0:T(8,128)(2,1)S(1)}, bf16[256,128]{1,0:T(8,128)(2,1)S(1)}, u32[]{:S(2)}, u32[]{:S(2)}) collective-permute-start(bf16[256,128]{1,0:T(8,128)(2,1)S(1)} %copy.54), channel_id=1, source_target_pairs={{248,0},{0,8},{8,16},{16,24},{24,32},{32,40},{40,48},{48,56},{56,6... | collective-permute-start | bytes 196616 | tf_op jit(solution)/shard_map/while/body/eval_jaxpr/ppermute | solution.py:14
  160.9 5.8 %collective-permute-start = (bf16[256,128]{1,0:T(8,128)(2,1)S(1)}, bf16[256,128]{1,0:T(8,128)(2,1)S(1)}, u32[]{:S(2)}, u32[]{:S(2)}) collective-permute-start(bf16[256,128]{1,0:T(8,128)(2,1)S(1)} %copy.53), channel_id=1, source_target_pairs={{248,0},{0,8},{8,16},{16,24},{24,32},{32,40},{40,48},{48,56},{56,6... | collective-permute-start | bytes 196616 | tf_op jit(solution)/shard_map/while/body/eval_jaxpr/ppermute | solution.py:14
  161.0 6.5 %collective-permute-start.1 = (bf16[256,128]{1,0:T(8,128)(2,1)S(1)}, bf16[256,128]{1,0:T(8,128)(2,1)S(1)}, u32[]{:S(2)}, u32[]{:S(2)}) collective-permute-start(bf16[256,128]{1,0:T(8,128)(2,1)S(1)} %copy.54), channel_id=1, source_target_pairs={{248,0},{0,8},{8,16},{16,24},{24,32},{32,40},{40,48},{48,56},{56,6... | collective-permute-start | bytes 196616 | tf_op jit(solution)/shard_map/while/body/eval_jaxpr/ppermute | solution.py:14
  167.4 5.8 %collective-permute-start = (bf16[256,128]{1,0:T(8,128)(2,1)S(1)}, bf16[256,128]{1,0:T(8,128)(2,1)S(1)}, u32[]{:S(2)}, u32[]{:S(2)}) collective-permute-start(bf16[256,128]{1,0:T(8,128)(2,1)S(1)} %copy.53), channel_id=1, source_target_pairs={{248,0},{0,8},{8,16},{16,24},{24,32},{32,40},{40,48},{48,56},{56,6... | collective-permute-start | bytes 196616 | tf_op jit(solution)/shard_map/while/body/eval_jaxpr/ppermute | solution.py:14
  167.5 6.5 %collective-permute-start.1 = (bf16[256,128]{1,0:T(8,128)(2,1)S(1)}, bf16[256,128]{1,0:T(8,128)(2,1)S(1)}, u32[]{:S(2)}, u32[]{:S(2)}) collective-permute-start(bf16[256,128]{1,0:T(8,128)(2,1)S(1)} %copy.54), channel_id=1, source_target_pairs={{248,0},{0,8},{8,16},{16,24},{24,32},{32,40},{40,48},{48,56},{56,6... | collective-permute-start | bytes 196616 | tf_op jit(solution)/shard_map/while/body/eval_jaxpr/ppermute | solution.py:14
  174.0 5.8 %collective-permute-start = (bf16[256,128]{1,0:T(8,128)(2,1)S(1)}, bf16[256,128]{1,0:T(8,128)(2,1)S(1)}, u32[]{:S(2)}, u32[]{:S(2)}) collective-permute-start(bf16[256,128]{1,0:T(8,128)(2,1)S(1)} %copy.53), channel_id=1, source_target_pairs={{248,0},{0,8},{8,16},{16,24},{24,32},{32,40},{40,48},{48,56},{56,6... | collective-permute-start | bytes 196616 | tf_op jit(solution)/shard_map/while/body/eval_jaxpr/ppermute | solution.py:14
  174.0 6.5 %collective-permute-start.1 = (bf16[256,128]{1,0:T(8,128)(2,1)S(1)}, bf16[256,128]{1,0:T(8,128)(2,1)S(1)}, u32[]{:S(2)}, u32[]{:S(2)}) collective-permute-start(bf16[256,128]{1,0:T(8,128)(2,1)S(1)} %copy.54), channel_id=1, source_target_pairs={{248,0},{0,8},{8,16},{16,24},{24,32},{32,40},{40,48},{48,56},{56,6... | collective-permute-start | bytes 196616 | tf_op jit(solution)/shard_map/while/body/eval_jaxpr/ppermute | solution.py:14
  180.5 5.8 %collective-permute-start = (bf16[256,128]{1,0:T(8,128)(2,1)S(1)}, bf16[256,128]{1,0:T(8,128)(2,1)S(1)}, u32[]{:S(2)}, u32[]{:S(2)}) collective-permute-start(bf16[256,128]{1,0:T(8,128)(2,1)S(1)} %copy.53), channel_id=1, source_target_pairs={{248,0},{0,8},{8,16},{16,24},{24,32},{32,40},{40,48},{48,56},{56,6... | collective-permute-start | bytes 196616 | tf_op jit(solution)/shard_map/while/body/eval_jaxpr/ppermute | solution.py:14
  180.5 6.5 %collective-permute-start.1 = (bf16[256,128]{1,0:T(8,128)(2,1)S(1)}, bf16[256,128]{1,0:T(8,128)(2,1)S(1)}, u32[]{:S(2)}, u32[]{:S(2)}) collective-permute-start(bf16[256,128]{1,0:T(8,128)(2,1)S(1)} %copy.54), channel_id=1, source_target_pairs={{248,0},{0,8},{8,16},{16,24},{24,32},{32,40},{40,48},{48,56},{56,6... | collective-permute-start | bytes 196616 | tf_op jit(solution)/shard_map/while/body/eval_jaxpr/ppermute | solution.py:14
  187.0 5.8 %collective-permute-start = (bf16[256,128]{1,0:T(8,128)(2,1)S(1)}, bf16[256,128]{1,0:T(8,128)(2,1)S(1)}, u32[]{:S(2)}, u32[]{:S(2)}) collective-permute-start(bf16[256,128]{1,0:T(8,128)(2,1)S(1)} %copy.53), channel_id=1, source_target_pairs={{248,0},{0,8},{8,16},{16,24},{24,32},{32,40},{40,48},{48,56},{56,6... | collective-permute-start | bytes 196616 | tf_op jit(solution)/shard_map/while/body/eval_jaxpr/ppermute | solution.py:14
  187.0 6.5 %collective-permute-start.1 = (bf16[256,128]{1,0:T(8,128)(2,1)S(1)}, bf16[256,128]{1,0:T(8,128)(2,1)S(1)}, u32[]{:S(2)}, u32[]{:S(2)}) collective-permute-start(bf16[256,128]{1,0:T(8,128)(2,1)S(1)} %copy.54), channel_id=1, source_target_pairs={{248,0},{0,8},{8,16},{16,24},{24,32},{32,40},{40,48},{48,56},{56,6... | collective-permute-start | bytes 196616 | tf_op jit(solution)/shard_map/while/body/eval_jaxpr/ppermute | solution.py:14
  193.5 5.8 %collective-permute-start = (bf16[256,128]{1,0:T(8,128)(2,1)S(1)}, bf16[256,128]{1,0:T(8,128)(2,1)S(1)}, u32[]{:S(2)}, u32[]{:S(2)}) collective-permute-start(bf16[256,128]{1,0:T(8,128)(2,1)S(1)} %copy.53), channel_id=1, source_target_pairs={{248,0},{0,8},{8,16},{16,24},{24,32},{32,40},{40,48},{48,56},{56,6... | collective-permute-start | bytes 196616 | tf_op jit(solution)/shard_map/while/body/eval_jaxpr/ppermute | solution.py:14
  193.5 6.5 %collective-permute-start.1 = (bf16[256,128]{1,0:T(8,128)(2,1)S(1)}, bf16[256,128]{1,0:T(8,128)(2,1)S(1)}, u32[]{:S(2)}, u32[]{:S(2)}) collective-permute-start(bf16[256,128]{1,0:T(8,128)(2,1)S(1)} %copy.54), channel_id=1, source_target_pairs={{248,0},{0,8},{8,16},{16,24},{24,32},{32,40},{40,48},{48,56},{56,6... | collective-permute-start | bytes 196616 | tf_op jit(solution)/shard_map/while/body/eval_jaxpr/ppermute | solution.py:14
  200.0 5.8 %collective-permute-start = (bf16[256,128]{1,0:T(8,128)(2,1)S(1)}, bf16[256,128]{1,0:T(8,128)(2,1)S(1)}, u32[]{:S(2)}, u32[]{:S(2)}) collective-permute-start(bf16[256,128]{1,0:T(8,128)(2,1)S(1)} %copy.53), channel_id=1, source_target_pairs={{248,0},{0,8},{8,16},{16,24},{24,32},{32,40},{40,48},{48,56},{56,6... | collective-permute-start | bytes 196616 | tf_op jit(solution)/shard_map/while/body/eval_jaxpr/ppermute | solution.py:14
  200.0 6.5 %collective-permute-start.1 = (bf16[256,128]{1,0:T(8,128)(2,1)S(1)}, bf16[256,128]{1,0:T(8,128)(2,1)S(1)}, u32[]{:S(2)}, u32[]{:S(2)}) collective-permute-start(bf16[256,128]{1,0:T(8,128)(2,1)S(1)} %copy.54), channel_id=1, source_target_pairs={{248,0},{0,8},{8,16},{16,24},{24,32},{32,40},{40,48},{48,56},{56,6... | collective-permute-start | bytes 196616 | tf_op jit(solution)/shard_map/while/body/eval_jaxpr/ppermute | solution.py:14
  (2 other events, 5.4 us)
where the time goes:
time: 226 us; the launch traced here: 223 us
  waiting for transfers between devices  127 us (56%)
  matrix products  44.7 us (20%)
  other arithmetic  26.2 us (12%)
  blocking collectives  12.9 us (6%)
  starting transfers between devices  4.67 us (2%)
  local copies, waits for them, and re-layouts  4.11 us (2%)
  loops' own time  3.46 us (2%)
    ppermute x62, waiting for transfers between devices, shifted(): return lax.ppermute(block, axis, route)  127 us
    dot_general x32, matrix products, attend(): jnp.einsum('cgqk,kcd->cgqd', weight_b, val_heads, preferred_element_type=...  29.9 us
    dot_general x32, matrix products, attend(): jnp.einsum('qcgd,kcd->cgqk', q_local, key_heads, preferred_element_type=j...  14.8 us
    reduce_sum x32, other arithmetic, attend(): total = total * factor + jnp.sum(weight, axis=-1)  14.2 us
    all_to_all x1, blocking collectives, body(): lax.all_to_all(local_out, 'head', split_axis=0, concat_axis=1, tiled=True)  12.9 us
    ppermute x62, starting transfers between devices, shifted(): return lax.ppermute(block, axis, route)  4.67 us
  transfers between devices with their start and end apart: 62, of which 62 were waited for; matrix products, arithmetic and copies ran while one was open for 31% of the time, Pallas kernels for 0%

commit v1 on v0

v1 whole, which is shorter than its diff:
```python
import functools
import math

import jax
import jax.numpy as jnp
from jax import lax
from jax.experimental import pallas as pl
from jax.experimental.pallas import tpu as pltpu
from jax.sharding import PartitionSpec as P

HD = 128
SPAN = 128
MOST = 4096
CHUNK = 256


def doc_start(lengths_ref, ndocs, pos):
    start, end = jnp.int32(0), jnp.int32(0)
    for d in range(ndocs):
        end = end + lengths_ref[d]
        start = jnp.where(pos >= end, end, start)
    return start


def attend_kernel(
    lengths_ref, order_ref, q_ref, kv_ref, out_ref,
    inverse, q_st, keys, vals, top, accum, bias, sems,
):
    ndocs = lengths_ref.shape[0]
    nspan = order_ref.shape[0]
    spans = q_ref.shape[0] // SPAN
    heads = q_ref.shape[1] // HD
    per = CHUNK // SPAN
    me = lax.axis_index("ctx")
    rate = math.log2(math.e) / math.sqrt(HD)

    @pl.loop(0, nspan)
    def _(i):
        inverse[order_ref[i]] = i

    def fetch(t, c, i):
        for j in range(per):
            slot = inverse[c * per + j]
            src = kv_ref.at[pl.ds(pl.multiple_of(slot * SPAN, SPAN), SPAN)]
            dst = pl.ds(pl.multiple_of(i * CHUNK + j * SPAN, SPAN), SPAN)
            pltpu.make_async_copy(src.at[:, :HD], keys.at[t, dst], sems.at[t, i, 0]).start()
            pltpu.make_async_copy(src.at[:, HD:], vals.at[t, dst, :HD], sems.at[t, i, 1]).start()

    last, count, whole = [], [], []
    for t in range(spans):
        p = order_ref[me * spans + t]
        first = doc_start(lengths_ref, ndocs, p * SPAN)
        inner = doc_start(lengths_ref, ndocs, p * SPAN + SPAN - 1)
        last.append(p)
        count.append(p // per - first // CHUNK + 1)
        whole.append(inner)

        @pl.loop(0, count[t])
        def _(i):
            fetch(t, p // per - i, i)

    for t in range(spans):
        for h in range(heads):
            q_st[t, h * SPAN : (h + 1) * SPAN] = q_ref[
                t * SPAN : (t + 1) * SPAN, h * HD : (h + 1) * HD
            ]
        vals[t, :, HD:] = jnp.ones((vals.shape[1], HD), jnp.bfloat16)

    for t in range(spans):
        p = last[t]
        row_pos = p * SPAN + lax.broadcasted_iota(jnp.int32, (SPAN, HD), 0)
        row_start = jnp.zeros((SPAN, HD), jnp.int32)
        end = jnp.int32(0)
        for d in range(ndocs):
            end = end + lengths_ref[d]
            row_start = jnp.where(row_pos >= end, end, row_start)

        def fold(i, masked, begin):
            rows = pl.ds(pl.multiple_of(i * CHUNK, CHUNK), CHUNK)
            if masked:
                for j in range(CHUNK // HD):
                    col = (p // per - i) * CHUNK + j * HD + lax.broadcasted_iota(
                        jnp.int32, (SPAN, HD), 1
                    )
                    ok = (col >= row_start) & (col <= row_pos)
                    bias[:, j * HD : (j + 1) * HD] = jnp.where(ok, 0.0, -1e30)
            kb = keys[t, rows]
            vb = vals[t, rows]
            for h in range(0, heads, 2):
                part = pl.ds(h * SPAN, 2 * SPAN)
                score = lax.dot_general(
                    q_st[t, part], kb, (((1,), (1,)), ((), ())),
                    preferred_element_type=jnp.float32,
                ) * rate
                if masked:
                    score = (score.reshape(2, SPAN, CHUNK) + bias[...][None]).reshape(2 * SPAN, CHUNK)
                best = jnp.max(score, axis=1, keepdims=True)
                if begin:
                    fresh = jnp.broadcast_to(best, (2 * SPAN, HD))
                else:
                    old = top[part]
                    fresh = jnp.maximum(old, best)
                weight = jnp.exp2(score - jnp.concatenate([fresh] * (CHUNK // HD), axis=1))
                made = jnp.dot(
                    weight.astype(jnp.bfloat16), vb, preferred_element_type=jnp.float32
                )
                top[part] = fresh
                if begin:
                    accum[part] = made
                else:
                    factor = jnp.exp2(old - fresh)
                    accum[part] = accum[part] * jnp.concatenate([factor, factor], axis=1) + made

        def arrive(i):
            rows = pl.ds(pl.multiple_of(i * CHUNK, CHUNK), CHUNK)
            pltpu.make_async_copy(kv_ref.at[pl.ds(0, CHUNK), :HD], keys.at[t, rows], sems.at[t, i, 0]).wait()
            pltpu.make_async_copy(kv_ref.at[pl.ds(0, CHUNK), HD:], vals.at[t, rows, :HD], sems.at[t, i, 1]).wait()

        arrive(0)
        fold(0, True, True)

        @pl.loop(1, count[t])
        def _(i):
            arrive(i)
            clear = (p // per - i) * CHUNK >= whole[t]

            @pl.when(clear)
            def _():
                fold(i, False, False)

            @pl.when(jnp.logical_not(clear))
            def _():
                fold(i, True, False)

        for h in range(heads):
            part = pl.ds(h * SPAN, SPAN)
            done = accum[part, :HD] / accum[part, HD:]
            out_ref[t * SPAN : (t + 1) * SPAN, h * HD : (h + 1) * HD] = done.astype(jnp.bfloat16)


def attend(queries, kv, doc_lengths, span_order):
    rows, width = queries.shape
    heads, spans = width // HD, rows // SPAN
    chunks = MOST // CHUNK + 1
    smem = pl.BlockSpec(memory_space=pltpu.SMEM)
    return pl.pallas_call(
        attend_kernel,
        out_shape=jax.ShapeDtypeStruct((rows, width), jnp.bfloat16),
        in_specs=[smem, smem, pl.BlockSpec(memory_space=pltpu.VMEM), pl.BlockSpec(memory_space=pl.ANY)],
        out_specs=pl.BlockSpec(memory_space=pltpu.VMEM),
        scratch_shapes=[
            pltpu.SMEM((span_order.shape[0],), jnp.int32),
            pltpu.VMEM((spans, heads * SPAN, HD), jnp.bfloat16),
            pltpu.VMEM((spans, chunks * CHUNK, HD), jnp.bfloat16),
            pltpu.VMEM((spans, chunks * CHUNK, 2 * HD), jnp.bfloat16),
            pltpu.VMEM((heads * SPAN, HD), jnp.float32),
            pltpu.VMEM((heads * SPAN, 2 * HD), jnp.float32),
            pltpu.VMEM((SPAN, CHUNK), jnp.float32),
            pltpu.SemaphoreType.DMA((spans, chunks, 2)),
        ],
        compiler_params=pltpu.CompilerParams(vmem_limit_bytes=40 * 2**20),
        name="attend",
    )(doc_lengths, span_order, queries, kv)


def body(queries, keys, values, doc_lengths, span_order):
    kv = jnp.concatenate([keys, values], axis=1)
    kv = lax.all_gather(kv, "ctx", axis=0, tiled=True)
    local_out = attend(queries, kv, doc_lengths, span_order)
    return lax.all_to_all(local_out, "head", split_axis=0, concat_axis=1, tiled=True)


def solution(mesh):
    return jax.shard_map(
        body,
        mesh=mesh,
        in_specs=(P("ctx", "head"), P("ctx", "head"), P("ctx", "head"), P(), P()),
        out_specs=P(("ctx", "head"), None),
        check_vma=False,
    )
```

time: 226 us -> 129 us (0.57)
  the two profiles are of different devices: /device:TPU:30 before, /device:TPU:97 now
where the time goes in v1:
time: 129 us
  waiting for transfers between devices  68.6 us (53%)
  Pallas kernels  24.4 us (19%)
  blocking collectives  15.3 us (12%)
  between operations  13.4 us (10%)
  local copies, waits for them, and re-layouts  5.37 us (4%)
  other arithmetic  1.54 us (1%)
    all_gather x1, waiting for transfers between devices, body(): kv = lax.all_gather(kv, 'ctx', axis=0, tiled=True)  68.6 us
    pallas_call x1, Pallas kernels, attend(): pl.pallas_call(attend_kernel, out_shape=jax.ShapeDtypeStruct((rows, width...  24.4 us
    all_to_all x1, blocking collectives, body(): lax.all_to_all(local_out, 'head', split_axis=0, concat_axis=1, tiled=True)  15.3 us
    unnamed x8, local copies, waits for them, and re-layouts  4.54 us
  transfers between devices with their start and end apart: 1, of which 1 were waited for; matrix products, arithmetic and copies ran while one was open for 0% of the time, Pallas kernels for 0%

profile of v1, /device:TPU:97, one launch (start us, length us, event | category | flops | bytes accessed | tf_op | source)
XLA Modules:
  0.0 128.6 jit_solution(17250767227488448317)
XLA Ops:
  6.5 0.0 all-gather.2.cloned.1.call-start
  6.5 1.5 %pad_maximum_fusion = bf16[256,256]{1,0:T(8,128)(2,1)} fusion(bf16[256,128]{1,0:T(8,128)(2,1)} %param.7, bf16[256,128]{1,0:T(8,128)(2,1)} %param.6), kind=kLoop, calls=%fused_computation | loop fusion | flops 262144 | bytes 262144 | tf_op jit(solution)/shard_map/concatenate | solution.py:167
  8.1 0.0 all-gather.2.cloned.1.call-update
  8.1 68.6 %all-gather.2.cloned.1.call-done.kv_ref = bf16[8192,256]{1,0:T(8,128)(2,1)} async-done(((bf16[256,256]{1,0:T(8,128)(2,1)}), bf16[8192,256]{1,0:T(8,128)(2,1)}) %all-gather.2.cloned.1.call-update) | async-done | bytes 4194320 | tf_op jit(solution)/shard_map/all_gather | solution.py:168
  76.7 0.0 copy-start
  76.7 2.2 %copy-done = bf16[8192,256]{1,0:T(8,128)(2,1)S(1)} copy-done((bf16[8192,256]{1,0:T(8,128)(2,1)S(1)}, bf16[8192,256]{1,0:T(8,128)(2,1)}, u32[]{:S(2)}) %copy-start) | copy-done | bytes 4194328
  78.9 0.0 copy-start.1
  78.9 1.0 copy-done.1
  79.9 0.0 copy-start.2
  79.9 0.7 copy-done.2
  80.6 0.0 copy-start.3
  80.6 0.7 copy-done.3
  81.2 24.4 %attend.1 = bf16[256,1024]{1,0:T(8,128)(2,1)S(1)} custom-call(s32[16]{0:T(128)S(1)} %copy-done.2, s32[64]{0:T(128)S(1)} %copy-done.3, bf16[256,1024]{1,0:T(8,128)(2,1)S(1)} %copy-done.1, bf16[8192,256]{1,0:T(8,128)(2,1)S(1)} %copy-done), custom_call_target="tpu_custom_call" | custom-call | tf_op jit(solution)/shard_map/attend/pallas_call | solution.py:146
  105.7 15.3 %all_to_all.19 = bf16[8,32,1024]{2,1,0:T(8,128)(2,1)S(1)} all-to-all(bf16[8,32,1024]{2,1,0:T(8,128)(2,1)S(1)} %bitcast.4), channel_id=1, replica_groups=mesh['ctx'=32,'head'=8] {'head'}, dimensions={0} | all-to-all | bytes 1048576 | tf_op jit(solution)/shard_map/all_to_all | solution.py:170
  121.0 0.8 copy.7
Async XLA Ops:
  6.5 70.2 %all-gather.2.cloned.1.call-start = ((), (), s32[]{:S(2)}) async-start(), calls=%async_computation.1 | async-start | bytes 4325376 | tf_op jit(solution)/shard_map/all_gather | solution.py:168
  76.7 2.2 %copy-start = (bf16[8192,256]{1,0:T(8,128)(2,1)S(1)}, bf16[8192,256]{1,0:T(8,128)(2,1)}, u32[]{:S(2)}) copy-start(bf16[8192,256]{1,0:T(8,128)(2,1)} %all-gather.2.cloned.1.call-done.kv_ref) | copy-start | bytes 12582916
  78.9 1.0 copy-start.1
  79.9 0.7 copy-start.2
  80.6 0.7 copy-start.3
Sparse Core Ops, SparseCore 0:
  9.2 67.4 all-gather.1

commit v2 on v1

--- a/solution.py
+++ b/solution.py
@@ -1,4 +1,3 @@
-import functools
 import math
 
 import jax
@@ -12,6 +11,8 @@
 SPAN = 128
 MOST = 4096
 CHUNK = 256
+DEPTH = 8
+MESH = pl.DeviceIdType.MESH
 
 
 def doc_start(lengths_ref, ndocs, pos):
@@ -23,9 +24,15 @@
 
 
 def attend_kernel(
-    lengths_ref, order_ref, q_ref, kv_ref, out_ref,
-    inverse, q_st, keys, vals, top, accum, bias, sems,
+    lengths_in, order_in, q_ref, k_ref, v_ref, out_ref,
+    lengths_ref, order_ref, inverse, q_st, keys, vals, top, accum, bias, sems, first_sems,
 ):
+    small = [
+        pltpu.make_async_copy(order_in, order_ref, first_sems.at[0]),
+        pltpu.make_async_copy(lengths_in, lengths_ref, first_sems.at[1]),
+    ]
+    for copy in small:
+        copy.start()
     ndocs = lengths_ref.shape[0]
     nspan = order_ref.shape[0]
     spans = q_ref.shape[0] // SPAN
@@ -34,6 +41,19 @@
     me = lax.axis_index("ctx")
     rate = math.log2(math.e) / math.sqrt(HD)
 
+    asked = []
+    for t in range(spans):
+        for h in range(heads):
+            copy = pltpu.make_async_copy(
+                q_ref.at[t * SPAN : (t + 1) * SPAN, h * HD : (h + 1) * HD],
+                q_st.at[t, h * SPAN : (h + 1) * SPAN],
+                first_sems.at[2 + t * heads + h],
+            )
+            copy.start()
+            asked.append(copy)
+    for copy in small:
+        copy.wait()
+
     @pl.loop(0, nspan)
     def _(i):
         inverse[order_ref[i]] = i
@@ -41,10 +61,10 @@
     def fetch(t, c, i):
         for j in range(per):
             slot = inverse[c * per + j]
-            src = kv_ref.at[pl.ds(pl.multiple_of(slot * SPAN, SPAN), SPAN)]
+            src = pl.ds(pl.multiple_of(slot * SPAN, SPAN), SPAN)
             dst = pl.ds(pl.multiple_of(i * CHUNK + j * SPAN, SPAN), SPAN)
-            pltpu.make_async_copy(src.at[:, :HD], keys.at[t, dst], sems.at[t, i, 0]).start()
-            pltpu.make_async_copy(src.at[:, HD:], vals.at[t, dst, :HD], sems.at[t, i, 1]).start()
+            pltpu.make_async_copy(k_ref.at[src], keys.at[t, dst], sems.at[t, i, 0]).start()
+            pltpu.make_async_copy(v_ref.at[src], vals.at[t, dst, :HD], sems.at[t, i, 1]).start()
 
     last, count, whole = [], [], []
     for t in range(spans):
@@ -60,12 +80,10 @@
             fetch(t, p // per - i, i)
 
     for t in range(spans):
-        for h in range(heads):
-            q_st[t, h * SPAN : (h + 1) * SPAN] = q_ref[
-                t * SPAN : (t + 1) * SPAN, h * HD : (h + 1) * HD
-            ]
         vals[t, :, HD:] = jnp.ones((vals.shape[1], HD), jnp.bfloat16)
 
+    for copy in asked:
+        copy.wait()
     for t in range(spans):
         p = last[t]
         row_pos = p * SPAN + lax.broadcasted_iota(jnp.int32, (SPAN, HD), 0)
@@ -113,8 +131,8 @@
 
         def arrive(i):
             rows = pl.ds(pl.multiple_of(i * CHUNK, CHUNK), CHUNK)
-            pltpu.make_async_copy(kv_ref.at[pl.ds(0, CHUNK), :HD], keys.at[t, rows], sems.at[t, i, 0]).wait()
-            pltpu.make_async_copy(kv_ref.at[pl.ds(0, CHUNK), HD:], vals.at[t, rows, :HD], sems.at[t, i, 1]).wait()
+            pltpu.make_async_copy(k_ref.at[pl.ds(0, CHUNK)], keys.at[t, rows], sems.at[t, i, 0]).wait()
+            pltpu.make_async_copy(v_ref.at[pl.ds(0, CHUNK)], vals.at[t, rows, :HD], sems.at[t, i, 1]).wait()
 
         arrive(0)
         fold(0, True, True)
@@ -138,17 +156,133 @@
             out_ref[t * SPAN : (t + 1) * SPAN, h * HD : (h + 1) * HD] = done.astype(jnp.bfloat16)
 
 
-def attend(queries, kv, doc_lengths, span_order):
+def gather_kernel(k_in, v_in, k_out, v_out, send, recv, here):
+    rows = k_in.shape[0]
+    half = rows // 2
+    me = lax.axis_index("ctx")
+    x, z, c = me // (2 * DEPTH), (me // 2) % DEPTH, me % 2
+
+    def block(xx, zz, cc):
+        return xx * (2 * DEPTH) + ((zz + 2 * DEPTH) % DEPTH) * 2 + cc
+
+    up, down = block(x, z + 1, c), block(x, z - 1, c)
+    across, beside = block(1 - x, z, c), block(x, z, 1 - c)
+
+    barrier = pltpu.get_barrier_semaphore()
+    for other in (up, down, across, beside):
+        pl.semaphore_signal(barrier, inc=1, device_id={"ctx": other}, device_id_type=MESH)
+    pl.semaphore_wait(barrier, 4)
+
+    own = pl.ds(pl.multiple_of(me * rows, rows), rows)
+    stay = [
+        pltpu.make_async_copy(k_in, k_out.at[own], here.at[0]),
+        pltpu.make_async_copy(v_in, v_out.at[own], here.at[1]),
+    ]
+    for copy in stay:
+        copy.start()
+
+    sent = []
+
+    def put(out, blk, first, count, to, kind, s, src=None):
+        place = out.at[pl.ds(pl.multiple_of(blk * rows + first, half), count)]
+        copy = pltpu.make_async_remote_copy(
+            src_ref=place if src is None else src.at[pl.ds(first, count)],
+            dst_ref=place,
+            send_sem=send.at[kind, s],
+            recv_sem=recv.at[kind, s],
+            device_id={"ctx": to},
+            device_id_type=MESH,
+        )
+        copy.start()
+        sent.append(copy)
+
+    def got(out, blk, first, count, kind, s):
+        place = out.at[pl.ds(pl.multiple_of(blk * rows + first, half), count)]
+        pltpu.make_async_remote_copy(
+            src_ref=place,
+            dst_ref=place,
+            send_sem=send.at[kind, s],
+            recv_sem=recv.at[kind, s],
+            device_id={"ctx": beside},
+            device_id_type=MESH,
+        ).wait_recv()
+
+    ways = ((k_out, k_in, up, -1, 0), (v_out, v_in, down, 1, 1))
+    for out, src, to, sign, i in ways:
+        put(out, me, 0, half, across, 6 + i, 0, src)
+        put(out, me, 0, rows, to, 0 + i, 0, src)
+    for out, src, to, sign, i in ways:
+        put(out, me, half, half, across, 4 + i, 0, src)
+        put(out, me, 0, rows, beside, 8 + i, 0, src)
+    for out, src, to, sign, i in ways:
+        blk = block(1 - x, z, c)
+        got(out, blk, 0, half, 6 + i, 0)
+        put(out, blk, 0, half, to, 2 + i, 0)
+        put(out, blk, 0, half, beside, 10 + i, 0)
+    for s in range(1, DEPTH):
+        for out, src, to, sign, i in ways:
+            blk = block(x, z + sign * s, c)
+            got(out, blk, 0, rows, 0 + i, s - 1)
+            if s < DEPTH - 1:
+                put(out, blk, 0, rows, to, 0 + i, s)
+            put(out, blk, half, half, across, 4 + i, s)
+            put(out, blk, 0, rows, beside, 8 + i, s)
+        for out, src, to, sign, i in ways:
+            blk = block(1 - x, z + sign * s, c)
+            got(out, blk, 0, half, 2 + i, s - 1)
+            if s < DEPTH - 1:
+                put(out, blk, 0, half, to, 2 + i, s)
+            put(out, blk, 0, half, beside, 10 + i, s)
+        for out, src, to, sign, i in ways:
+            blk = block(1 - x, z + sign * (s - 1), c)
+            got(out, blk, half, half, 4 + i, s - 1)
+            put(out, blk, half, half, beside, 12 + i, s - 1)
+    for out, src, to, sign, i in ways:
+        blk = block(1 - x, z + sign * (DEPTH - 1), c)
+        got(out, blk, half, half, 4 + i, DEPTH - 1)
+        put(out, blk, half, half, beside, 12 + i, DEPTH - 1)
+    for s in range(DEPTH):
+        for out, src, to, sign, i in ways:
+            got(out, block(x, z + sign * s, 1 - c), 0, rows, 8 + i, s)
+            got(out, block(1 - x, z + sign * s, 1 - c), 0, half, 10 + i, s)
+            got(out, block(1 - x, z + sign * s, 1 - c), half, half, 12 + i, s)
+    for copy in sent:
+        copy.wait_send()
+    for copy in stay:
+        copy.wait()
+
+
+def gather(keys, values):
+    rows, width = keys.shape
+    whole = jax.ShapeDtypeStruct((rows * lax.axis_size("ctx"), width), keys.dtype)
+    return pl.pallas_call(
+        gather_kernel,
+        out_shape=(whole, whole),
+        in_specs=[pl.BlockSpec(memory_space=pltpu.HBM)] * 2,
+        out_specs=(pl.BlockSpec(memory_space=pltpu.HBM),) * 2,
+        scratch_shapes=[
+            pltpu.SemaphoreType.DMA((14, DEPTH)),
+            pltpu.SemaphoreType.DMA((14, DEPTH)),
+            pltpu.SemaphoreType.DMA((2,)),
+        ],
+        compiler_params=pltpu.CompilerParams(collective_id=0, has_side_effects=True),
+        name="gather",
+    )(keys, values)
+
+
+def attend(queries, keys, values, doc_lengths, span_order):
     rows, width = queries.shape
     heads, spans = width // HD, rows // SPAN
     chunks = MOST // CHUNK + 1
-    smem = pl.BlockSpec(memory_space=pltpu.SMEM)
+    hbm = pl.BlockSpec(memory_space=pltpu.HBM)
     return pl.pallas_call(
         attend_kernel,
         out_shape=jax.ShapeDtypeStruct((rows, width), jnp.bfloat16),
-        in_specs=[smem, smem, pl.BlockSpec(memory_space=pltpu.VMEM), pl.BlockSpec(memory_space=pl.ANY)],
+        in_specs=[hbm] * 5,
         out_specs=pl.BlockSpec(memory_space=pltpu.VMEM),
         scratch_shapes=[
+            pltpu.SMEM(doc_lengths.shape, jnp.int32),
+            pltpu.SMEM(span_order.shape, jnp.int32),
             pltpu.SMEM((span_order.shape[0],), jnp.int32),
             pltpu.VMEM((spans, heads * SPAN, HD), jnp.bfloat16),
             pltpu.VMEM((spans, chunks * CHUNK, HD), jnp.bfloat16),
@@ -157,16 +291,16 @@
             pltpu.VMEM((heads * SPAN, 2 * HD), jnp.float32),
             pltpu.VMEM((SPAN, CHUNK), jnp.float32),
             pltpu.SemaphoreType.DMA((spans, chunks, 2)),
+            pltpu.SemaphoreType.DMA((2 + spans * heads,)),
         ],
         compiler_params=pltpu.CompilerParams(vmem_limit_bytes=40 * 2**20),
         name="attend",
-    )(doc_lengths, span_order, queries, kv)
+    )(doc_lengths, span_order, queries, keys, values)
 
 
 def body(queries, keys, values, doc_lengths, span_order):
-    kv = jnp.concatenate([keys, values], axis=1)
-    kv = lax.all_gather(kv, "ctx", axis=0, tiled=True)
-    local_out = attend(queries, kv, doc_lengths, span_order)
+    keys, values = gather(keys, values)
+    local_out = attend(queries, keys, values, doc_lengths, span_order)
     return lax.all_to_all(local_out, "head", split_axis=0, concat_axis=1, tiled=True)
 
 

time: 129 us -> 82.1 us (0.64)
  waiting for transfers between devices: 68.6 us -> 0 us
  Pallas kernels: 24.4 us -> 60 us
  between operations: 13.4 us -> 0.03 us
  other arithmetic: 1.54 us -> 0 us
    all_gather x1 -> x0, waiting for transfers between devices: 68.6 us -> none  [body(): kv = lax.all_gather(kv, 'ctx', axis=0, tiled=True)]
    pallas_call x0 -> x1, Pallas kernels: none -> 38.4 us  [gather(): pl.pallas_call(gather_kernel, out_shape=(whole, whole), in_specs=[pl.Bloc...]
    pallas_call x1, Pallas kernels: 24.4 us -> 21.6 us  [attend(): pl.pallas_call(attend_kernel, out_shape=jax.ShapeDtypeStruct((rows, width...]
    concatenate x1 -> x0, other arithmetic: 1.54 us -> none  [body(): kv = jnp.concatenate([keys, values], axis=1)]
    unnamed x8 -> x10, local copies, waits for them, and re-layouts: 4.54 us -> 5.53 us
  transfers between devices with their start and end apart: 1 -> 0, of which waited for: 1 -> 0; matrix products, arithmetic and copies ran while one was open for 0% -> 0% of each run, Pallas kernels for 0% -> 0%
where the time goes in v2:
time: 82.1 us; the launch traced here: 81.8 us
  Pallas kernels  60 us (73%)
  blocking collectives  15.4 us (19%)
  local copies, waits for them, and re-layouts  6.36 us (8%)
    pallas_call x1, Pallas kernels, gather(): pl.pallas_call(gather_kernel, out_shape=(whole, whole), in_specs=[pl.Bloc...  38.4 us
    pallas_call x1, Pallas kernels, attend(): pl.pallas_call(attend_kernel, out_shape=jax.ShapeDtypeStruct((rows, width...  21.6 us
    all_to_all x1, blocking collectives, body(): lax.all_to_all(local_out, 'head', split_axis=0, concat_axis=1, tiled=True)  15.4 us
    unnamed x10, local copies, waits for them, and re-layouts  5.53 us

profile of v2, /device:TPU:97, one launch (start us, length us, event | category | flops | bytes accessed | tf_op | source)
XLA Modules:
  0.0 81.8 jit_solution(17025145821572208525)
XLA Ops:
  0.0 38.4 %gather.1 = (bf16[8192,128]{1,0:T(8,128)(2,1)}, bf16[8192,128]{1,0:T(8,128)(2,1)}) custom-call(bf16[256,128]{1,0:T(8,128)(2,1)} %k_in.1, bf16[256,128]{1,0:T(8,128)(2,1)} %v_in.1), custom_call_target="tpu_custom_call" | custom-call | tf_op jit(solution)/shard_map/gather/pallas_call | solution.py:258
  38.4 0.0 copy-start
  38.4 1.6 %copy-done = bf16[8192,128]{1,0:T(8,128)(2,1)S(1)} copy-done((bf16[8192,128]{1,0:T(8,128)(2,1)S(1)}, bf16[8192,128]{1,0:T(8,128)(2,1)}, u32[]{:S(2)}) %copy-start) | copy-done | bytes 2097176
  40.0 0.0 copy-start.1
  40.0 1.6 %copy-done.1 = bf16[8192,128]{1,0:T(8,128)(2,1)S(1)} copy-done((bf16[8192,128]{1,0:T(8,128)(2,1)S(1)}, bf16[8192,128]{1,0:T(8,128)(2,1)}, u32[]{:S(2)}) %copy-start.1) | copy-done | bytes 2097176
  41.6 0.0 copy-start.2
  41.6 1.0 %copy-done.2 = bf16[256,1024]{1,0:T(8,128)(2,1)S(1)} copy-done((bf16[256,1024]{1,0:T(8,128)(2,1)S(1)}, bf16[256,1024]{1,0:T(8,128)(2,1)}, u32[]{:S(2)}) %copy-start.2) | copy-done | bytes 524312
  42.7 0.0 copy-start.3
  42.7 0.7 copy-done.3
  43.3 0.0 copy-start.4
  43.3 0.7 copy-done.4
  44.0 21.6 %attend.1 = bf16[256,1024]{1,0:T(8,128)(2,1)S(1)} custom-call(s32[16]{0:T(128)S(1)} %copy-done.3, s32[64]{0:T(128)S(1)} %copy-done.4, bf16[256,1024]{1,0:T(8,128)(2,1)S(1)} %copy-done.2, bf16[8192,128]{1,0:T(8,128)(2,1)S(1)} %copy-done, bf16[8192,128]{1,0:T(8,128)(2,1)S(1)} %copy-done.1), custom_call_target="tpu_custom_call" | custom-call | tf_op jit(solution)/shard_map/attend/pallas_call | solution.py:278
  65.6 15.4 %all_to_all.19 = bf16[8,32,1024]{2,1,0:T(8,128)(2,1)S(1)} all-to-all(bf16[8,32,1024]{2,1,0:T(8,128)(2,1)S(1)} %bitcast.4), channel_id=1, replica_groups=mesh['ctx'=32,'head'=8] {'head'}, dimensions={0} | all-to-all | bytes 1048576 | tf_op jit(solution)/shard_map/all_to_all | solution.py:304
  81.0 0.8 %copy.7 = bf16[8,4,8,1024]{3,2,0,1:T(8,128)(2,1)} copy(bf16[8,4,8,1024]{3,2,1,0:T(8,128)(2,1)S(1)} %bitcast.5) | data formatting | bytes 1048576 | tf_op jit(solution)/shard_map/all_to_all | solution.py:304
Async XLA Ops:
  38.4 1.6 %copy-start = (bf16[8192,128]{1,0:T(8,128)(2,1)S(1)}, bf16[8192,128]{1,0:T(8,128)(2,1)}, u32[]{:S(2)}) copy-start(bf16[8192,128]{1,0:T(8,128)(2,1)} %get-tuple-element.7.k_ref) | copy-start | bytes 6291460
  40.0 1.6 %copy-start.1 = (bf16[8192,128]{1,0:T(8,128)(2,1)S(1)}, bf16[8192,128]{1,0:T(8,128)(2,1)}, u32[]{:S(2)}) copy-start(bf16[8192,128]{1,0:T(8,128)(2,1)} %get-tuple-element.8.v_ref) | copy-start | bytes 6291460
  41.6 1.0 %copy-start.2 = (bf16[256,1024]{1,0:T(8,128)(2,1)S(1)}, bf16[256,1024]{1,0:T(8,128)(2,1)}, u32[]{:S(2)}) copy-start(bf16[256,1024]{1,0:T(8,128)(2,1)} %q_ref.1) | copy-start | bytes 1572868
  42.7 0.7 copy-start.3
  43.3 0.7 copy-start.4

commit v3 on v0

v3 whole, which is shorter than its diff:
```python
import math

import jax
import jax.numpy as jnp
from jax import lax
from jax.experimental import pallas as pl
from jax.experimental.pallas import tpu as pltpu
from jax.sharding import PartitionSpec as P

HD = 128
SPAN = 128
DEPTH = 8
CHUNK = 512
NCHUNK = 16
FAR = -(2.0**100)
RATE = math.log2(math.e) / math.sqrt(HD)
MESH = pl.DeviceIdType.MESH
RING, CROSS, BESIDE = 0, 24, 36
KIND = {"V": 0, "K": 1, "P": 2}


def kernel(
    lengths_ref, order_ref, q_ref, k_in, v_in, out_ref,
    buf, qa, acc, top, ka, va, s0, s1, row_pos, row_start, o_st,
    send, recv, o_send, o_recv, here, q_sem,
):
    rows = k_in.shape[0]
    spans = rows // SPAN
    heads = q_ref.shape[1] // HD
    group = heads * SPAN
    width = q_ref.shape[1]
    nheads = lax.axis_size("head")
    share = rows // nheads
    ndocs = lengths_ref.shape[0]
    me = lax.axis_index("ctx")
    my_head = lax.axis_index("head")
    x, z, c = me // (2 * DEPTH), (me // 2) % DEPTH, me % 2
    sign = 1 - 2 * c

    def block(px, dz, flip):
        xx = x + px - 2 * x * px
        cc = c + flip - 2 * c * flip
        return xx * (2 * DEPTH) + ((z + dz + 2 * DEPTH) % DEPTH) * 2 + cc

    up, down, across, beside = block(0, 1, 0), block(0, -1, 0), block(1, 0, 0), block(0, 0, 1)
    far_to, far_from = block(0, sign, 0), {0: block(0, -3 * sign, 0), 1: block(1, -3 * sign, 0)}
    near = {
        (px, dz, f): block(px, dz, f) for px in (0, 1) for dz in range(-3, 5) for f in (0, 1)
    }

    barrier = pltpu.get_barrier_semaphore()
    for other in (up, down, across, beside):
        pl.semaphore_signal(barrier, inc=1, device_id={"ctx": other}, device_id_type=MESH)
    for j in range(1, nheads):
        pl.semaphore_signal(
            barrier, inc=1, device_id={"head": lax.rem(my_head + j, nheads)}, device_id_type=MESH
        )

    K, V, KV = (0, rows), (rows, rows), (0, 2 * rows)
    PART = {"V": V, "K": K, "P": K}
    PX = {"V": 0, "K": 0, "P": 1}

    def place(blk, part):
        return buf.at[pl.ds(pl.multiple_of(blk * (2 * rows) + part[0], rows), part[1])]

    stay = [
        pltpu.make_async_copy(k_in, place(me, K), here.at[0]),
        pltpu.make_async_copy(v_in, place(me, V), here.at[1]),
    ]
    asked = []
    for t in range(spans):
        for h in range(heads):
            asked.append(
                pltpu.make_async_copy(
                    q_ref.at[t * SPAN : (t + 1) * SPAN, h * HD : (h + 1) * HD],
                    qa.at[t * group + h * SPAN : t * group + (h + 1) * SPAN, 0:HD],
                    q_sem.at[t * heads + h],
                )
            )
    for copy in stay + asked:
        copy.start()

    sent = {}

    def put(blk, part, to, sem, src=None):
        place_there = place(blk, part)
        pltpu.make_async_remote_copy(
            src_ref=place_there if src is None else src,
            dst_ref=place_there,
            send_sem=send.at[sem],
            recv_sem=recv.at[sem],
            device_id={"ctx": to},
            device_id_type=MESH,
        ).start()
        sent[sem] = part

    def mirror(blk, part, sem):
        spot = place(blk, part)
        return pltpu.make_async_remote_copy(
            src_ref=spot,
            dst_ref=spot,
            send_sem=send.at[sem],
            recv_sem=recv.at[sem],
            device_id={"ctx": beside},
            device_id_type=MESH,
        )

    def got(blk, part, sem):
        mirror(blk, part, sem).wait_recv()

    ways = ((0, up, 1), (1, down, -1))

    def ring(kind, s, way):
        return RING + (s - 1) * 6 + KIND[kind] * 2 + way

    def step_of(s, way):
        return 1 + (s - 1) * 2 + way

    def onward(kind, s):
        for way, to, d in ways:
            blk = near[PX[kind], -d * s, 0]
            got(blk, PART[kind], ring(kind, s, way))
            if s < 3:
                put(blk, PART[kind], to, ring(kind, s + 1, way))
            if kind == "V":
                put(blk, V, across, CROSS + 1 + step_of(s, way))
        if s == 3:
            put(far_from[PX[kind]], PART[kind], far_to, ring(kind, 4, 0))
        for way, to, d in ways:
            blk = near[PX[kind], -d * s, 0]
            if kind == "K":
                put(blk, KV, beside, BESIDE + step_of(s, way))
            if kind == "P":
                put(blk, K, beside, BESIDE + 8 + step_of(s, way))

    def crossed(s):
        for way, to, d in ways:
            blk = near[1, -d * s, 0]
            got(blk, V, CROSS + 1 + step_of(s, way))
            put(blk, V, beside, BESIDE + 16 + step_of(s, way))

    def last(kind):
        blk = near[PX[kind], 4, 0]
        got(blk, PART[kind], ring(kind, 4, 0))
        if kind == "V":
            put(blk, V, across, CROSS + 8)
        if kind == "K":
            put(blk, KV, beside, BESIDE + 7)
        if kind == "P":
            put(blk, K, beside, BESIDE + 8 + 7)

    def crossed_last():
        got(near[1, 4, 0], V, CROSS + 8)
        put(near[1, 4, 0], V, beside, BESIDE + 16 + 7)

    def crossed_first():
        got(near[1, 0, 0], V, CROSS + 1)
        put(near[1, 0, 0], V, beside, BESIDE + 16)

    def need_own(s):
        for way, to, d in ways:
            got(near[0, -d * s, 1], KV, BESIDE + step_of(s, way))

    def need_other(s):
        for way, to, d in ways:
            got(near[1, -d * s, 1], K, BESIDE + 8 + step_of(s, way))
            got(near[1, -d * s, 1], V, BESIDE + 16 + step_of(s, way))

    def need_first():
        got(near[1, 0, 1], K, BESIDE + 8)
        got(near[1, 0, 1], V, BESIDE + 16)

    def need_last():
        got(near[0, 4, 1], KV, BESIDE + 7)
        got(near[1, 4, 1], K, BESIDE + 8 + 7)
        got(near[1, 4, 1], V, BESIDE + 16 + 7)

    middle = {
        0: [crossed_first, need_first],
        1: [lambda: onward("K", 1)],
        2: [lambda: need_own(1)],
        3: [lambda: onward("V", 2)],
        4: [lambda: need_other(1)],
        5: [lambda: crossed(2)],
        6: [lambda: need_own(2), lambda: onward("K", 3)],
        7: [lambda: crossed(3)],
        8: [lambda: need_other(2), lambda: last("K")],
        10: [lambda: need_own(3)],
    }
    finish = {
        0: [lambda: onward("V", 1)],
        1: [lambda: onward("P", 1)],
        2: [lambda: crossed(1)],
        3: [lambda: onward("K", 2)],
        4: [lambda: onward("P", 2)],
        5: [lambda: onward("V", 3)],
        6: [lambda: onward("P", 3)],
        7: [lambda: last("V")],
        8: [lambda: last("P")],
        9: [crossed_last],
        11: [lambda: need_other(3)],
        12: [need_last],
    }

    def chunk_blocks(m):
        s, k = (m + 2) // 4, (m + 2) % 4
        e0, e4 = 1 - (s + 3) // 4, s // 4
        mid = 1 - e0 - e4
        low, high = k % 2, k // 2
        flip = (1 - e0) * low
        return (
            block(e0 * low + mid * high, -s, flip),
            block(e0 * low + e4 + mid * high, s, e0 + flip),
        )

    def prepare(m):
        slot = m % 4
        for j, blk in enumerate(chunk_blocks(m)):
            base = pl.multiple_of(blk * (2 * rows), 2 * rows)
            va[pl.ds(pl.multiple_of(slot * CHUNK + j * rows, rows), rows), 0:HD] = buf[
                pl.ds(base + rows, rows)
            ]
            keys = buf[pl.ds(base, rows)]
            for t in range(spans):
                first = pl.multiple_of((slot * spans + t) * CHUNK + j * rows, rows)
                ka[pl.ds(first, rows), 0:HD] = keys
                for i in range(spans):
                    pos = order_ref[blk * spans + i] * SPAN + lax.broadcasted_iota(
                        jnp.int32, (SPAN, SPAN), 0
                    )
                    ok = (pos >= row_start[t, 0:1]) & (pos <= row_pos[t, 0:1])
                    ka[pl.ds(first + i * SPAN, SPAN), HD:] = jnp.where(ok, 0.0, FAR).astype(
                        jnp.bfloat16
                    )

    def scores(m, t, dest):
        first = pl.multiple_of(((m % 4) * spans + t) * CHUNK, CHUNK)
        dest[...] = lax.dot_general(
            qa[pl.ds(pl.multiple_of(t * group, group), group)],
            ka[pl.ds(first, CHUNK)],
            (((1,), (1,)), ((), ())),
            preferred_element_type=jnp.float32,
        )

    def fold(m, t, source):
        part = pl.ds(pl.multiple_of(t * group, group), group)
        score = source[...]
        old = top[part]
        new = jnp.maximum(old, jnp.max(score, axis=1, keepdims=True))
        weight = jnp.exp2((score - jnp.concatenate([new] * (CHUNK // HD), axis=1)) * RATE)
        factor = jnp.exp2((old - new) * RATE)
        made = jnp.dot(
            weight.astype(jnp.bfloat16),
            va[pl.ds(pl.multiple_of((m % 4) * CHUNK, CHUNK), CHUNK)],
            preferred_element_type=jnp.float32,
        )
        top[part] = new
        acc[part] = acc[part] * jnp.concatenate([factor, factor], axis=1) + made

    def hand_out(t):
        for h in range(heads):
            part = slice(t * group + h * SPAN, t * group + (h + 1) * SPAN)
            done = acc[part, 0:HD] / acc[part, HD:]
            o_st[t * SPAN : (t + 1) * SPAN, h * HD : (h + 1) * HD] = done.astype(jnp.bfloat16)
        columns = pl.ds(pl.multiple_of(my_head * width, width), width)
        for r in range(SPAN // share):
            j = t * (SPAN // share) + r
            source = o_st.at[j * share : (j + 1) * share]

            @pl.when(my_head != j)
            def _():
                pltpu.make_async_remote_copy(
                    src_ref=source,
                    dst_ref=out_ref.at[:, columns],
                    send_sem=o_send.at[j],
                    recv_sem=o_recv.at[my_head],
                    device_id={"head": j},
                    device_id_type=MESH,
                ).start()

            @pl.when(my_head == j)
            def _():
                pltpu.make_async_copy(source, out_ref.at[:, columns], here.at[2]).start()

    pl.semaphore_wait(barrier, 4 + nheads - 1)
    put(me, K, across, CROSS + 0, k_in)
    for way, to, d in ways:
        put(me, V, to, ring("V", 1, way), v_in)
    put(me, V, across, CROSS + 1, v_in)
    for way, to, d in ways:
        put(me, K, to, ring("K", 1, way), k_in)
    for copy in stay:
        copy.wait()
    put(me, KV, beside, BESIDE + 0)

    eye = (
        lax.broadcasted_iota(jnp.int32, (SPAN, SPAN), 0)
        == lax.broadcasted_iota(jnp.int32, (SPAN, SPAN), 1)
    ).astype(jnp.bfloat16)
    for t in range(spans):
        pos = order_ref[me * spans + t] * SPAN + lax.broadcasted_iota(jnp.int32, (8, SPAN), 1)
        start, end = jnp.zeros((8, SPAN), jnp.int32), jnp.int32(0)
        for d in range(ndocs):
            end = end + lengths_ref[d]
            start = jnp.where(pos >= end, end, start)
        row_pos[t], row_start[t] = pos, start
        for h in range(heads):
            qa[t * group + h * SPAN : t * group + (h + 1) * SPAN, HD:] = eye
    va[:, HD:] = jnp.ones((va.shape[0], HD), jnp.bfloat16)
    acc[...] = jnp.zeros_like(acc)
    top[...] = jnp.full(top.shape, -1e30, jnp.float32)
    for copy in asked:
        copy.wait()

    got(near[1, 0, 0], K, CROSS + 0)
    for way, to, d in ways:
        put(near[1, 0, 0], K, to, ring("P", 1, way))
    put(near[1, 0, 0], K, beside, BESIDE + 8)
    got(near[0, 0, 1], KV, BESIDE + 0)
    prepare(0)
    scores(0, 0, s0)

    @pl.loop(0, NCHUNK)
    def _(u):
        tail = u // 12
        v = (u - 12) * tail
        t_a = tail * (v // 2)
        t_b = 1 - tail + t_a
        m_a = (1 - tail) * u + tail * (12 + 2 * (v % 2))
        m_b = m_a + tail
        nxt = v + 1
        early = (1 - tail) * (u + 1)
        t_n = tail * ((nxt // 2) % 2)
        m_n = early + tail * (12 + 2 * (nxt % 2))
        m_p = early + tail * (14 + (v + 2) // 3)
        scores(m_b, t_b, s1)
        fold(m_a, t_a, s0)
        for key, jobs in middle.items():

            @pl.when(u == key)
            def _(jobs=jobs):
                for job in jobs:
                    job()

        @pl.when(u < 13)
        def _():
            prepare(m_p)

        scores(m_n, t_n, s0)
        fold(m_b, t_b, s1)
        for key, jobs in finish.items():

            @pl.when(u == key)
            def _(jobs=jobs):
                for job in jobs:
                    job()

        @pl.when(u == 11)
        def _():
            prepare(13)

        @pl.when(u == 12)
        def _():
            prepare(15)

        @pl.when(u == 13)
        def _():
            hand_out(0)

    hand_out(1)
    for sem, part in sent.items():
        mirror(me, part, sem).wait_send()

    columns = pl.ds(pl.multiple_of(my_head * width, width), width)
    for j in range(nheads):
        source = o_st.at[j * share : (j + 1) * share]
        landing = pltpu.make_async_remote_copy(
            src_ref=source,
            dst_ref=out_ref.at[:, j * width : (j + 1) * width],
            send_sem=o_send.at[j],
            recv_sem=o_recv.at[j],
            device_id={"head": j},
            device_id_type=MESH,
        )

        @pl.when(my_head != j)
        def _():
            landing.wait_recv()
            landing.wait_send()

        @pl.when(my_head == j)
        def _():
            pltpu.make_async_copy(source, out_ref.at[:, columns], here.at[2]).wait()


def body(queries, keys, values, doc_lengths, span_order):
    rows, width = queries.shape
    heads, spans = width // HD, rows // SPAN
    n_ctx, nheads = lax.axis_size("ctx"), lax.axis_size("head")
    group = heads * SPAN
    smem, hbm = pl.BlockSpec(memory_space=pltpu.SMEM), pl.BlockSpec(memory_space=pltpu.HBM)
    f32, bf16, i32 = jnp.float32, jnp.bfloat16, jnp.int32
    return pl.pallas_call(
        kernel,
        out_shape=jax.ShapeDtypeStruct((rows // nheads, width * nheads), bf16),
        in_specs=[smem, smem, hbm, hbm, hbm],
        out_specs=hbm,
        scratch_shapes=[
            pltpu.VMEM((n_ctx * 2 * rows, HD), bf16),
            pltpu.VMEM((spans * group, 2 * HD), bf16),
            pltpu.VMEM((spans * group, 2 * HD), f32),
            pltpu.VMEM((spans * group, HD), f32),
            pltpu.VMEM((4 * spans * CHUNK, 2 * HD), bf16),
            pltpu.VMEM((4 * CHUNK, 2 * HD), bf16),
            pltpu.VMEM((group, CHUNK), f32),
            pltpu.VMEM((group, CHUNK), f32),
            pltpu.VMEM((spans, 8, SPAN), i32),
            pltpu.VMEM((spans, 8, SPAN), i32),
            pltpu.VMEM((rows, width), bf16),
            pltpu.SemaphoreType.DMA((60,)),
            pltpu.SemaphoreType.DMA((60,)),
            pltpu.SemaphoreType.DMA((nheads,)),
            pltpu.SemaphoreType.DMA((nheads,)),
            pltpu.SemaphoreType.DMA((3,)),
            pltpu.SemaphoreType.DMA((spans * heads,)),
        ],
        compiler_params=pltpu.CompilerParams(
            collective_id=0, has_side_effects=True, vmem_limit_bytes=60 * 2**20
        ),
        name="attend",
    )(doc_lengths, span_order, queries, keys, values)


def solution(mesh):
    return jax.shard_map(
        body,
        mesh=mesh,
        in_specs=(P("ctx", "head"), P("ctx", "head"), P("ctx", "head"), P(), P()),
        out_specs=P(("ctx", "head"), None),
        check_vma=False,
    )
```

time: 226 us -> 62.8 us (0.28); the launches traced: 223 us -> 62.6 us
  waiting for transfers between devices: 127 us -> 0 us
  Pallas kernels: 0 us -> 60.7 us
  matrix products: 44.7 us -> 0 us
  other arithmetic: 26.2 us -> 0 us
  blocking collectives: 12.9 us -> 0 us
  starting transfers between devices: 4.67 us -> 0 us
  loops' own time: 3.46 us -> 0 us
    ppermute x62 -> x0, waiting for transfers between devices: 127 us -> none  [shifted(): return lax.ppermute(block, axis, route)]
    pallas_call x0 -> x1, Pallas kernels: none -> 60.7 us  [body(): pl.pallas_call(kernel, out_shape=jax.ShapeDtypeStruct((rows // nheads, wi...]
    dot_general x64 -> x0, matrix products: 44.7 us -> none  [the longest x32 29.9 us: attend(): jnp.einsum('cgqk,kcd->cgqd', weight_b, val_heads, preferred_element_type=...]
    reduce_sum x96 -> x0, other arithmetic: 20 us -> none  [the longest x32 14.2 us: attend(): total = total * factor + jnp.sum(weight, axis=-1)]
    all_to_all x1 -> x0, blocking collectives: 12.9 us -> none  [body(): lax.all_to_all(local_out, 'head', split_axis=0, concat_axis=1, tiled=True)]
    ppermute x62 -> x0, starting transfers between devices: 4.67 us -> none  [shifted(): return lax.ppermute(block, axis, route)]
    and x32 -> x0, other arithmetic: 4.49 us -> none  [fold_block(): (q_doc[:, None] == k_doc[None, :]) & (k_pos[None, :] <= q_pos[:, None])]
    another operation x1 -> x0, loops' own time: 3.46 us -> none  [body(): lax.fori_loop(0, n_ctx - 1, circle_step, (initial, keys, values))]
  transfers between devices with their start and end apart: 62 -> 0, of which waited for: 62 -> 0; matrix products, arithmetic and copies ran while one was open for 31% -> 0% of each run, Pallas kernels for 0% -> 0%
where the time goes in v3:
time: 62.8 us; the launch traced here: 62.6 us
  Pallas kernels  60.7 us (97%)
  local copies, waits for them, and re-layouts  1.87 us (3%)
    pallas_call x1, Pallas kernels, body(): pl.pallas_call(kernel, out_shape=jax.ShapeDtypeStruct((rows // nheads, wi...  60.7 us
    unnamed x1, local copies, waits for them, and re-layouts  1.87 us

profile of v3, /device:TPU:30, one launch (start us, length us, event | category | flops | bytes accessed | tf_op | source)
XLA Modules:
  0.0 62.6 jit_solution(7796026647862874088)
XLA Ops:
  0.0 60.7 %attend.1 = bf16[32,8192]{1,0:T(8,128)(2,1)} custom-call(s32[16]{0:T(128)} %lengths_ref.1, s32[64]{0:T(128)} %order_ref.1, bf16[256,1024]{1,0:T(8,128)(2,1)} %q_ref.1, bf16[256,128]{1,0:T(8,128)(2,1)} %k_in.1, bf16[256,128]{1,0:T(8,128)(2,1)} %v_in.1), custom_call_target="tpu_custom_call" | custom-call | tf_op jit(solution)/shard_map/attend/pallas_call | solution.py:403
  60.7 1.9 %copy.7 = bf16[32,8192]{1,0:T(8,128)(2,1)} copy(bf16[32,8192]{1,0:T(8,128)(2,1)} %attend.1) | data formatting | bytes 1048576

commit v4 on v3

v4 whole, which is shorter than its diff:
```python
import math

import jax
import jax.numpy as jnp
from jax import lax
from jax.experimental import pallas as pl
from jax.experimental.pallas import tpu as pltpu
from jax.sharding import PartitionSpec as P

HD = 128
SPAN = 128
DEPTH = 8
CHUNK = 512
NCHUNK = 16
FAR = -(2.0**100)
RATE = math.log2(math.e) / math.sqrt(HD)
MESH = pl.DeviceIdType.MESH
VALS, KEYS, GUEST, FIRST, OVER, SIDE = 0, 7, 14, 21, 23, 30


def _pair(p, s, flip):
    return ((p, -s, flip), (p, s, flip))


ORDER = (
    ((0, 0, 0), (0, 0, 1)), _pair(0, 1, 0), ((1, 0, 0), (1, 0, 1)), _pair(0, 1, 1),
    _pair(0, 2, 0), _pair(1, 1, 0), _pair(0, 2, 1), _pair(1, 1, 1),
    _pair(0, 3, 0), _pair(1, 2, 0), _pair(0, 3, 1), _pair(1, 2, 1),
    _pair(1, 3, 0), _pair(1, 3, 1), ((0, 4, 0), (1, 4, 0)), ((0, 4, 1), (1, 4, 1)),
)


def kernel(
    lengths_ref, order_ref, q_ref, k_in, v_in, out_ref,
    buf, qa, acc, top, bias, s0, s1, row_pos, row_start, o_st,
    send, recv, o_send, o_recv, here, q_sem,
):
    rows = k_in.shape[0]
    spans = rows // SPAN
    heads = q_ref.shape[1] // HD
    group = heads * SPAN
    width = q_ref.shape[1]
    nheads = lax.axis_size("head")
    n_ctx = lax.axis_size("ctx")
    share = rows // nheads
    ndocs = lengths_ref.shape[0]
    me = lax.axis_index("ctx")
    my_head = lax.axis_index("head")
    x, z, c = me // (2 * DEPTH), (me // 2) % DEPTH, me % 2
    sign = 1 - 2 * c

    def block(px, dz, flip):
        xx = x + px - 2 * x * px
        cc = c + flip - 2 * c * flip
        return xx * (2 * DEPTH) + ((z + dz + 2 * DEPTH) % DEPTH) * 2 + cc

    across, beside = block(1, 0, 0), block(0, 0, 1)
    hop = {0: block(0, 1, 0), 1: block(0, -1, 0)}
    far_to, far_from = block(0, sign, 0), {p: block(p, -3 * sign, 0) for p in (0, 1)}
    near = {
        (px, dz, f): block(px, dz, f) for px in (0, 1) for dz in range(-3, 5) for f in (0, 1)
    }

    barrier = pltpu.get_barrier_semaphore()
    for other in (*hop.values(), across, beside):
        pl.semaphore_signal(barrier, inc=1, device_id={"ctx": other}, device_id_type=MESH)
    for j in range(1, nheads):
        pl.semaphore_signal(
            barrier, inc=1, device_id={"head": lax.rem(my_head + j, nheads)}, device_id_type=MESH
        )

    K, V, KV = (0, rows), (rows, rows), (0, 2 * rows)

    def place(blk, part):
        return buf.at[pl.ds(pl.multiple_of(blk * (2 * rows) + part[0], rows), part[1])]

    stay = [
        pltpu.make_async_copy(k_in, place(me, K), here.at[0]),
        pltpu.make_async_copy(v_in, place(me, V), here.at[1]),
    ]
    asked = []
    for t in range(spans):
        for h in range(heads):
            asked.append(
                pltpu.make_async_copy(
                    q_ref.at[t * SPAN : (t + 1) * SPAN, h * HD : (h + 1) * HD],
                    qa.at[t * group + h * SPAN : t * group + (h + 1) * SPAN, 0:HD],
                    q_sem.at[t * heads + h],
                )
            )
    for copy in stay + asked:
        copy.start()

    sent = {}

    def put(blk, part, to, sem):
        place_there = place(blk, part)
        pltpu.make_async_remote_copy(
            src_ref=place_there,
            dst_ref=place_there,
            send_sem=send.at[sem],
            recv_sem=recv.at[sem],
            device_id={"ctx": to},
            device_id_type=MESH,
        ).start()
        sent[sem] = part

    def mirror(blk, part, sem):
        spot = place(blk, part)
        return pltpu.make_async_remote_copy(
            src_ref=spot,
            dst_ref=spot,
            send_sem=send.at[sem],
            recv_sem=recv.at[sem],
            device_id={"ctx": beside},
            device_id_type=MESH,
        )

    def got(blk, part, sem):
        mirror(blk, part, sem).wait_recv()

    ways = ((0, 1), (1, -1))

    def of(first, s, way):
        return first + (s - 1) * 2 + way

    RIDES = {"V": (0, V, VALS), "K": (0, K, KEYS), "P": (1, K, GUEST)}

    def ride(kind, s):
        p, part, first = RIDES[kind]
        if s == 4:
            got(near[p, 4, 0], part, first + 6)
            if kind == "V":
                put(near[0, 4, 0], V, across, OVER + 6)
            return
        for w, d in ways:
            blk = near[p, -s * d, 0]
            got(blk, part, of(first, s, w))
            if s < 3:
                put(blk, part, hop[w], of(first, s + 1, w))
        if s == 3:
            put(far_from[p], part, far_to, first + 6)
        if kind == "V":
            for w, d in ways:
                put(near[0, -s * d, 0], V, across, of(OVER, s, w))

    def pass_own(s):
        if s == 4:
            put(near[0, 4, 0], KV, beside, SIDE + 7)
            return
        for w, d in ways:
            put(near[0, -s * d, 0], KV, beside, SIDE + of(1, s, w))

    def guest_0():
        got(near[1, 0, 0], K, FIRST)
        for w, d in ways:
            put(near[1, 0, 0], K, hop[w], of(GUEST, 1, w))

    def other(s):
        if s == 0:
            got(near[1, 0, 0], V, FIRST + 1)
            put(near[1, 0, 0], KV, beside, SIDE + 8)
        elif s == 4:
            got(near[1, 4, 0], V, OVER + 6)
            put(near[1, 4, 0], KV, beside, SIDE + 8 + 7)
        else:
            for w, d in ways:
                blk = near[1, -s * d, 0]
                got(blk, V, of(OVER, s, w))
                put(blk, KV, beside, SIDE + 8 + of(1, s, w))

    def side(p, s):
        if s == 0:
            got(near[p, 0, 1], KV, SIDE + 8 * p)
        elif s == 4:
            got(near[p, 4, 1], KV, SIDE + 8 * p + 7)
        else:
            for w, d in ways:
                got(near[p, -d * s, 1], KV, SIDE + 8 * p + of(1, s, w))

    middle = {
        0: [guest_0, lambda: ride("V", 1), lambda: other(0), lambda: ride("K", 1), lambda: pass_own(1)],
        1: [lambda: side(1, 0)],
        2: [lambda: side(0, 1)],
        3: [lambda: ride("K", 2), lambda: pass_own(2)],
        5: [lambda: side(0, 2)],
        6: [lambda: ride("P", 3), lambda: side(1, 1)],
        7: [lambda: ride("K", 4), lambda: pass_own(4)],
        9: [lambda: ride("P", 4), lambda: other(4), lambda: side(0, 3)],
        10: [lambda: side(1, 2)],
    }
    finish = {
        1: [lambda: ride("P", 1)],
        2: [lambda: ride("V", 2), lambda: other(1)],
        3: [lambda: ride("P", 2)],
        4: [lambda: ride("V", 3)],
        5: [lambda: ride("K", 3), lambda: other(2), lambda: pass_own(3)],
        6: [lambda: ride("V", 4)],
        7: [lambda: other(3)],
        11: [lambda: side(1, 3)],
        12: [lambda: side(0, 4), lambda: side(1, 4)],
    }

    def chunk_blocks(m):
        def digit(code):
            return lax.rem(lax.shift_right_logical(jnp.int32(code), m), 2)

        found = []
        for i in range(2):
            px, far, flip = ([ORDER[n][i][f] for n in range(NCHUNK)] for f in range(3))
            dz = sum(
                (1 << e) * digit(sum(((v % DEPTH) >> e & 1) << n for n, v in enumerate(far)))
                for e in range(3)
            )
            code = [sum(v << n for n, v in enumerate(row)) for row in (px, flip)]
            found.append(block(digit(code[0]), dz, digit(code[1])))
        return found

    def keys_of(m, t):
        parts = []
        for blk in chunk_blocks(m):
            base = pl.multiple_of(blk * (2 * rows), 2 * rows)
            hide = pl.multiple_of(t * (rows * n_ctx) + blk * rows, rows)
            parts.append(jnp.concatenate([buf[pl.ds(base, rows)], bias[pl.ds(hide, rows)]], axis=1))
        return jnp.concatenate(parts, axis=0)

    def values_of(m):
        parts = []
        for blk in chunk_blocks(m):
            base = pl.multiple_of(blk * (2 * rows) + rows, rows)
            parts.append(
                jnp.concatenate([buf[pl.ds(base, rows)], jnp.ones((rows, HD), jnp.bfloat16)], axis=1)
            )
        return jnp.concatenate(parts, axis=0)

    def scores(m, t, dest):
        dest[...] = lax.dot_general(
            qa[pl.ds(pl.multiple_of(t * group, group), group)],
            keys_of(m, t),
            (((1,), (1,)), ((), ())),
            preferred_element_type=jnp.float32,
        )

    def fold(m, t, source):
        part = pl.ds(pl.multiple_of(t * group, group), group)
        score = source[...]
        old = top[part]
        new = jnp.maximum(old, jnp.max(score, axis=1, keepdims=True))
        weight = jnp.exp2((score - jnp.concatenate([new] * (CHUNK // HD), axis=1)) * RATE)
        factor = jnp.exp2((old - new) * RATE)
        made = jnp.dot(
            weight.astype(jnp.bfloat16), values_of(m), preferred_element_type=jnp.float32
        )
        top[part] = new
        acc[part] = acc[part] * jnp.concatenate([factor, factor], axis=1) + made

    def hand_out(t):
        for h in range(heads):
            part = slice(t * group + h * SPAN, t * group + (h + 1) * SPAN)
            done = acc[part, 0:HD] / acc[part, HD:]
            o_st[t * SPAN : (t + 1) * SPAN, h * HD : (h + 1) * HD] = done.astype(jnp.bfloat16)
        columns = pl.ds(pl.multiple_of(my_head * width, width), width)
        for r in range(SPAN // share):
            j = t * (SPAN // share) + r
            source = o_st.at[j * share : (j + 1) * share]

            @pl.when(my_head != j)
            def _():
                pltpu.make_async_remote_copy(
                    src_ref=source,
                    dst_ref=out_ref.at[:, columns],
                    send_sem=o_send.at[j],
                    recv_sem=o_recv.at[my_head],
                    device_id={"head": j},
                    device_id_type=MESH,
                ).start()

            @pl.when(my_head == j)
            def _():
                pltpu.make_async_copy(source, out_ref.at[:, columns], here.at[2]).start()

    eye = (
        lax.broadcasted_iota(jnp.int32, (SPAN, SPAN), 0)
        == lax.broadcasted_iota(jnp.int32, (SPAN, SPAN), 1)
    ).astype(jnp.bfloat16)
    for t in range(spans):
        pos = order_ref[me * spans + t] * SPAN + lax.broadcasted_iota(jnp.int32, (8, SPAN), 1)
        start, end = jnp.zeros((8, SPAN), jnp.int32), jnp.int32(0)
        for d in range(ndocs):
            end = end + lengths_ref[d]
            start = jnp.where(pos >= end, end, start)
        row_pos[t], row_start[t] = pos, start
        for h in range(heads):
            qa[t * group + h * SPAN : t * group + (h + 1) * SPAN, HD:] = eye
    acc[...] = jnp.zeros_like(acc)
    top[...] = jnp.full(top.shape, -1e30, jnp.float32)

    pl.semaphore_wait(barrier, 4 + nheads - 1)
    for copy in stay:
        copy.wait()
    put(me, K, across, FIRST)
    for w, d in ways:
        put(me, V, hop[w], of(VALS, 1, w))
    put(me, V, across, FIRST + 1)
    for w, d in ways:
        put(me, K, hop[w], of(KEYS, 1, w))
    put(me, KV, beside, SIDE)

    @pl.loop(0, n_ctx * spans, unroll=4)
    def _(i):
        pos = order_ref[i] * SPAN + lax.broadcasted_iota(jnp.int32, (SPAN, SPAN), 0)
        for t in range(spans):
            ok = (pos >= row_start[t, 0:1]) & (pos <= row_pos[t, 0:1])
            spot = pl.multiple_of(t * (rows * n_ctx) + i * SPAN, SPAN)
            bias[pl.ds(spot, SPAN)] = jnp.where(ok, 0.0, FAR).astype(jnp.bfloat16)

    for copy in asked:
        copy.wait()

    side(0, 0)
    scores(0, 0, s0)

    @pl.loop(0, NCHUNK)
    def _(u):
        tail = u // 12
        v = (u - 12) * tail
        t_a = tail * (v // 2)
        t_b = 1 - tail + t_a
        m_a = (1 - tail) * u + tail * (12 + 2 * (v % 2))
        m_b = m_a + tail
        nxt = v + 1
        early = (1 - tail) * (u + 1)
        t_n = tail * ((nxt // 2) % 2)
        m_n = early + tail * (12 + 2 * (nxt % 2))
        scores(m_b, t_b, s1)
        fold(m_a, t_a, s0)
        for key, jobs in middle.items():

            @pl.when(u == key)
            def _(jobs=jobs):
                for job in jobs:
                    job()

        scores(m_n, t_n, s0)
        fold(m_b, t_b, s1)
        for key, jobs in finish.items():

            @pl.when(u == key)
            def _(jobs=jobs):
                for job in jobs:
                    job()

        @pl.when(u == 13)
        def _():
            hand_out(0)

    hand_out(1)
    for sem, part in sent.items():
        mirror(me, part, sem).wait_send()

    columns = pl.ds(pl.multiple_of(my_head * width, width), width)
    for j in range(nheads):
        source = o_st.at[j * share : (j + 1) * share]
        landing = pltpu.make_async_remote_copy(
            src_ref=source,
            dst_ref=out_ref.at[:, j * width : (j + 1) * width],
            send_sem=o_send.at[j],
            recv_sem=o_recv.at[j],
            device_id={"head": j},
            device_id_type=MESH,
        )

        @pl.when(my_head != j)
        def _():
            landing.wait_recv()
            landing.wait_send()

        @pl.when(my_head == j)
        def _():
            pltpu.make_async_copy(source, out_ref.at[:, columns], here.at[2]).wait()


def body(queries, keys, values, doc_lengths, span_order):
    rows, width = queries.shape
    heads, spans = width // HD, rows // SPAN
    n_ctx, nheads = lax.axis_size("ctx"), lax.axis_size("head")
    group = heads * SPAN
    smem, hbm = pl.BlockSpec(memory_space=pltpu.SMEM), pl.BlockSpec(memory_space=pltpu.HBM)
    f32, bf16, i32 = jnp.float32, jnp.bfloat16, jnp.int32
    return pl.pallas_call(
        kernel,
        out_shape=jax.ShapeDtypeStruct((rows // nheads, width * nheads), bf16),
        in_specs=[smem, smem, hbm, hbm, hbm],
        out_specs=hbm,
        scratch_shapes=[
            pltpu.VMEM((n_ctx * 2 * rows, HD), bf16),
            pltpu.VMEM((spans * group, 2 * HD), bf16),
            pltpu.VMEM((spans * group, 2 * HD), f32),
            pltpu.VMEM((spans * group, HD), f32),
            pltpu.VMEM((spans * n_ctx * rows, HD), bf16),
            pltpu.VMEM((group, CHUNK), f32),
            pltpu.VMEM((group, CHUNK), f32),
            pltpu.VMEM((spans, 8, SPAN), i32),
            pltpu.VMEM((spans, 8, SPAN), i32),
            pltpu.VMEM((rows, width), bf16),
            pltpu.SemaphoreType.DMA((SIDE + 16,)),
            pltpu.SemaphoreType.DMA((SIDE + 16,)),
            pltpu.SemaphoreType.DMA((nheads,)),
            pltpu.SemaphoreType.DMA((nheads,)),
            pltpu.SemaphoreType.DMA((3,)),
            pltpu.SemaphoreType.DMA((spans * heads,)),
        ],
        compiler_params=pltpu.CompilerParams(
            collective_id=0, has_side_effects=True, vmem_limit_bytes=60 * 2**20
        ),
        name="attend",
    )(doc_lengths, span_order, queries, keys, values)


def solution(mesh):
    return jax.shard_map(
        body,
        mesh=mesh,
        in_specs=(P("ctx", "head"), P("ctx", "head"), P("ctx", "head"), P(), P()),
        out_specs=P(("ctx", "head"), None),
        check_vma=False,
    )
```

time: 62.8 us -> 55.9 us (0.89)
  Pallas kernels: 60.7 us -> 53.8 us
    pallas_call x1, Pallas kernels: 60.7 us -> 53.8 us  [body(): pl.pallas_call(kernel, out_shape=jax.ShapeDtypeStruct((rows // nheads, wi...]
where the time goes in v4:
time: 55.9 us; the launch traced here: 55.7 us
  Pallas kernels  53.8 us (96%)
  local copies, waits for them, and re-layouts  1.87 us (3%)
    pallas_call x1, Pallas kernels, body(): pl.pallas_call(kernel, out_shape=jax.ShapeDtypeStruct((rows // nheads, wi...  53.8 us
    unnamed x1, local copies, waits for them, and re-layouts  1.87 us

profile of v4, /device:TPU:30, one launch (start us, length us, event | category | flops | bytes accessed | tf_op | source)
XLA Modules:
  0.0 55.7 jit_solution(16362403417824861416)
XLA Ops:
  0.0 53.8 %attend.1 = bf16[32,8192]{1,0:T(8,128)(2,1)} custom-call(s32[16]{0:T(128)} %lengths_ref.1, s32[64]{0:T(128)} %order_ref.1, bf16[256,1024]{1,0:T(8,128)(2,1)} %q_ref.1, bf16[256,128]{1,0:T(8,128)(2,1)} %k_in.1, bf16[256,128]{1,0:T(8,128)(2,1)} %v_in.1), custom_call_target="tpu_custom_call" | custom-call | tf_op jit(solution)/shard_map/attend/pallas_call | solution.py:390
  53.9 1.9 %copy.7 = bf16[32,8192]{1,0:T(8,128)(2,1)} copy(bf16[32,8192]{1,0:T(8,128)(2,1)} %attend.1) | data formatting | bytes 1048576

commit v5 on v4

--- a/solution.py
+++ b/solution.py
@@ -23,16 +23,28 @@
 
 
 ORDER = (
-    ((0, 0, 0), (0, 0, 1)), _pair(0, 1, 0), ((1, 0, 0), (1, 0, 1)), _pair(0, 1, 1),
-    _pair(0, 2, 0), _pair(1, 1, 0), _pair(0, 2, 1), _pair(1, 1, 1),
-    _pair(0, 3, 0), _pair(1, 2, 0), _pair(0, 3, 1), _pair(1, 2, 1),
-    _pair(1, 3, 0), _pair(1, 3, 1), ((0, 4, 0), (1, 4, 0)), ((0, 4, 1), (1, 4, 1)),
+    ((0, 0, 0), (0, 0, 1)),
+    _pair(0, 1, 0),
+    ((1, 0, 0), (1, 0, 1)),
+    _pair(0, 1, 1),
+    _pair(0, 2, 0),
+    _pair(1, 1, 0),
+    _pair(0, 2, 1),
+    _pair(1, 1, 1),
+    _pair(0, 3, 0),
+    _pair(1, 2, 0),
+    _pair(0, 3, 1),
+    _pair(1, 2, 1),
+    _pair(1, 3, 0),
+    _pair(1, 3, 1),
+    ((0, 4, 0), (1, 4, 0)),
+    ((0, 4, 1), (1, 4, 1)),
 )
 
 
 def kernel(
     lengths_ref, order_ref, q_ref, k_in, v_in, out_ref,
-    buf, qa, acc, top, bias, s0, s1, row_pos, row_start, o_st,
+    buf, qa, acc, top, s0, s1, row_pos, row_start, o_st,
     send, recv, o_send, o_recv, here, q_sem,
 ):
     rows = k_in.shape[0]
@@ -41,7 +53,6 @@
     group = heads * SPAN
     width = q_ref.shape[1]
     nheads = lax.axis_size("head")
-    n_ctx = lax.axis_size("ctx")
     share = rows // nheads
     ndocs = lengths_ref.shape[0]
     me = lax.axis_index("ctx")
@@ -181,22 +192,21 @@
     middle = {
         0: [guest_0, lambda: ride("V", 1), lambda: other(0), lambda: ride("K", 1), lambda: pass_own(1)],
         1: [lambda: side(1, 0)],
-        2: [lambda: side(0, 1)],
+        2: [lambda: ride("P", 1), lambda: side(0, 1)],
         3: [lambda: ride("K", 2), lambda: pass_own(2)],
-        5: [lambda: side(0, 2)],
-        6: [lambda: ride("P", 3), lambda: side(1, 1)],
-        7: [lambda: ride("K", 4), lambda: pass_own(4)],
-        9: [lambda: ride("P", 4), lambda: other(4), lambda: side(0, 3)],
-        10: [lambda: side(1, 2)],
+        4: [lambda: ride("P", 2)],
+        5: [lambda: ride("V", 3), lambda: side(0, 2)],
+        6: [lambda: side(1, 1)],
+        7: [lambda: ride("V", 4)],
+        8: [lambda: other(3)],
+        9: [lambda: side(0, 3)],
+        10: [lambda: ride("P", 4), lambda: other(4), lambda: side(1, 2)],
     }
     finish = {
-        1: [lambda: ride("P", 1)],
         2: [lambda: ride("V", 2), lambda: other(1)],
-        3: [lambda: ride("P", 2)],
-        4: [lambda: ride("V", 3)],
         5: [lambda: ride("K", 3), lambda: other(2), lambda: pass_own(3)],
-        6: [lambda: ride("V", 4)],
-        7: [lambda: other(3)],
+        6: [lambda: ride("P", 3)],
+        7: [lambda: ride("K", 4), lambda: pass_own(4)],
         11: [lambda: side(1, 3)],
         12: [lambda: side(0, 4), lambda: side(1, 4)],
     }
@@ -217,11 +227,17 @@
         return found
 
     def keys_of(m, t):
+        first, stop = row_start[pl.ds(t, 1), 0], row_pos[pl.ds(t, 1), 0]
         parts = []
         for blk in chunk_blocks(m):
             base = pl.multiple_of(blk * (2 * rows), 2 * rows)
-            hide = pl.multiple_of(t * (rows * n_ctx) + blk * rows, rows)
-            parts.append(jnp.concatenate([buf[pl.ds(base, rows)], bias[pl.ds(hide, rows)]], axis=1))
+            for i in range(spans):
+                pos = order_ref[blk * spans + i] * SPAN + lax.broadcasted_iota(
+                    jnp.int32, (SPAN, SPAN), 0
+                )
+                ok = (pos >= first) & (pos <= stop)
+                hide = jnp.where(ok, 0.0, FAR).astype(jnp.bfloat16)
+                parts.append(jnp.concatenate([buf[pl.ds(base + i * SPAN, SPAN)], hide], axis=1))
         return jnp.concatenate(parts, axis=0)
 
     def values_of(m):
@@ -305,14 +321,6 @@
     for w, d in ways:
         put(me, K, hop[w], of(KEYS, 1, w))
     put(me, KV, beside, SIDE)
-
-    @pl.loop(0, n_ctx * spans, unroll=4)
-    def _(i):
-        pos = order_ref[i] * SPAN + lax.broadcasted_iota(jnp.int32, (SPAN, SPAN), 0)
-        for t in range(spans):
-            ok = (pos >= row_start[t, 0:1]) & (pos <= row_pos[t, 0:1])
-            spot = pl.multiple_of(t * (rows * n_ctx) + i * SPAN, SPAN)
-            bias[pl.ds(spot, SPAN)] = jnp.where(ok, 0.0, FAR).astype(jnp.bfloat16)
 
     for copy in asked:
         copy.wait()
@@ -397,7 +405,6 @@
             pltpu.VMEM((spans * group, 2 * HD), bf16),
             pltpu.VMEM((spans * group, 2 * HD), f32),
             pltpu.VMEM((spans * group, HD), f32),
-            pltpu.VMEM((spans * n_ctx * rows, HD), bf16),
             pltpu.VMEM((group, CHUNK), f32),
             pltpu.VMEM((group, CHUNK), f32),
             pltpu.VMEM((spans, 8, SPAN), i32),

time: 55.9 us -> 54.7 us (0.979)
  Pallas kernels: 53.8 us -> 52.6 us
    pallas_call x1, Pallas kernels: 53.8 us -> 52.6 us  [body(): pl.pallas_call(kernel, out_shape=jax.ShapeDtypeStruct((rows // nheads, wi...]
where the time goes in v5:
time: 54.7 us; the launch traced here: 54.5 us
  Pallas kernels  52.6 us (96%)
  local copies, waits for them, and re-layouts  1.87 us (3%)
    pallas_call x1, Pallas kernels, body(): pl.pallas_call(kernel, out_shape=jax.ShapeDtypeStruct((rows // nheads, wi...  52.6 us
    unnamed x1, local copies, waits for them, and re-layouts  1.87 us

profile of v5, /device:TPU:30, one launch (start us, length us, event | category | flops | bytes accessed | tf_op | source)
XLA Modules:
  0.0 54.5 jit_solution(6428062566547394366)
XLA Ops:
  0.0 52.6 %attend.1 = bf16[32,8192]{1,0:T(8,128)(2,1)} custom-call(s32[16]{0:T(128)} %lengths_ref.1, s32[64]{0:T(128)} %order_ref.1, bf16[256,1024]{1,0:T(8,128)(2,1)} %q_ref.1, bf16[256,128]{1,0:T(8,128)(2,1)} %k_in.1, bf16[256,128]{1,0:T(8,128)(2,1)} %v_in.1), custom_call_target="tpu_custom_call" | custom-call | tf_op jit(solution)/shard_map/attend/pallas_call | solution.py:398
  52.6 1.9 %copy.7 = bf16[32,8192]{1,0:T(8,128)(2,1)} copy(bf16[32,8192]{1,0:T(8,128)(2,1)} %attend.1) | data formatting | bytes 1048576

commit v6 on v5

--- a/solution.py
+++ b/solution.py
@@ -190,7 +190,7 @@
                 got(near[p, -d * s, 1], KV, SIDE + 8 * p + of(1, s, w))
 
     middle = {
-        0: [guest_0, lambda: ride("V", 1), lambda: other(0), lambda: ride("K", 1), lambda: pass_own(1)],
+        0: [lambda: ride("V", 1), lambda: ride("K", 1), lambda: other(0), lambda: pass_own(1)],
         1: [lambda: side(1, 0)],
         2: [lambda: ride("P", 1), lambda: side(0, 1)],
         3: [lambda: ride("K", 2), lambda: pass_own(2)],
@@ -325,6 +325,7 @@
     for copy in asked:
         copy.wait()
 
+    guest_0()
     side(0, 0)
     scores(0, 0, s0)
 

time: 54.7 us -> 55.8 us (1.020); the launches traced: 54.5 us -> 55 us
  no operation moved by 1% of the time
where the time goes in v6:
time: 55.8 us; the launch traced here: 55 us
  Pallas kernels  53.1 us (95%)
  local copies, waits for them, and re-layouts  1.87 us (3%)
    pallas_call x1, Pallas kernels, body(): pl.pallas_call(kernel, out_shape=jax.ShapeDtypeStruct((rows // nheads, wi...  53.1 us
    unnamed x1, local copies, waits for them, and re-layouts  1.87 us

profile of v6, /device:TPU:30, one launch (start us, length us, event | category | flops | bytes accessed | tf_op | source)
XLA Modules:
  0.0 55.0 jit_solution(5362147541976185652)
XLA Ops:
  0.0 53.1 %attend.1 = bf16[32,8192]{1,0:T(8,128)(2,1)} custom-call(s32[16]{0:T(128)} %lengths_ref.1, s32[64]{0:T(128)} %order_ref.1, bf16[256,1024]{1,0:T(8,128)(2,1)} %q_ref.1, bf16[256,128]{1,0:T(8,128)(2,1)} %k_in.1, bf16[256,128]{1,0:T(8,128)(2,1)} %v_in.1), custom_call_target="tpu_custom_call" | custom-call | tf_op jit(solution)/shard_map/attend/pallas_call | solution.py:399
  53.1 1.9 %copy.7 = bf16[32,8192]{1,0:T(8,128)(2,1)} copy(bf16[32,8192]{1,0:T(8,128)(2,1)} %attend.1) | data formatting | bytes 1048576
